TPU v7x, 32 devices: a whole 2x2x4 slice. The times are simulated.
32 devices in a mesh: groups: 2 (over y), space: 4 (over z), tm: 2 (over x), obs: 2 (over core).
Axes of the slice: x: 2, y: 2, z: 4, core: 2. Of those that a mesh axis runs over, the one named last changes fastest.
Arguments:
- state: bfloat16 [2048, 16384], P(('groups', 'tm', 'obs'), 'space'), parts along dimension 0, may hold values from -6 to 6
- spatial_factor: bfloat16 [16384, 16384], P(('tm', 'obs'), 'space'), may hold values from -0.0625 to 0.0625
- time_factor: bfloat16 [1024, 1024], P('space'), as said below
- footprints: bfloat16 [64, 48, 2048], P(('groups', 'space'), None, ('tm', 'obs')), parts along dimension 0, may hold values from -0.0390625 to 0.0390625
- tile_obs: int32 [64, 4], P(('groups', 'space'), ('tm', 'obs')), parts along dimension 0, may hold values from 0 to 31
- tile_block: int32 [64, 4], P(('groups', 'space'), ('tm', 'obs')), parts along dimension 0, may hold values from 0 to 7
- tile_hour: int32 [64, 4], P(('groups', 'space'), ('tm', 'obs')), parts along dimension 0, may hold values from 0 to 976, as said below
- tile_count: int32 [8, 4], P(('groups', 'space'), ('tm', 'obs')), parts along dimension 0, may hold values from 1 to 8, as said below
- obs_weight: float32 [64], P('groups'), parts along dimension 0, may hold values from 10 to 100
Outputs:
- hessian_product: float32 [2048, 16384], P(('groups', 'tm', 'obs'), 'space'), parts along dimension 0
There are 2 independent parts, one for each index of `groups`. A program takes and returns all parts, laid end to end along the dimension named above; an argument that names none is the same for every part. Nothing has to cross between parts.
Inputs may be any that keep to these rules, and one draw needn't show every extreme that they name: time_factor is symmetric. `tile_hour`: the tiles of row r start in the block of hours r // 8, hours (r // 8) * 256 to (r // 8) * 256 + 255. `tile_count`: the live slots are the first ones of each owner and block of hours; some entry equals 8.
All inputs are finite; a program needn't handle non-finite values.
Results may differ from a plain program's by a relative error of at most 0.019.
Values may be sent and summed in bfloat16 or wider, within the bound.
A program may use at most 128 MiB of HBM per device.

v0:
```python
import jax
import jax.numpy as jnp
from jax import lax
from jax.sharding import PartitionSpec as P


def from_behind(value, axis, steps):
    count = lax.axis_size(axis)
    leading, last = (max(0, -steps), min(count, count - steps))
    return lax.ppermute(value, axis, [(source, source + steps) for source in range(leading, last)])


def per_device(
    state,
    spatial_factor,
    time_factor,
    footprints,
    tile_obs,
    tile_block,
    tile_hour,
    tile_count,
    obs_weight,
):
    block_hours = time_factor.shape[0]
    cell_rows = spatial_factor.shape[0]
    slots = footprints.shape[0]
    lags = footprints.shape[1]
    width = footprints.shape[2]
    observations = obs_weight.shape[0]
    whole_factor = lax.all_gather(time_factor, "space", axis=0, tiled=True)
    full_state = lax.all_gather(state, ("tm", "obs"), axis=0, tiled=True)
    picked = full_state
    mixed = lax.psum_scatter(
        lax.dot_general(
            picked, spatial_factor, (((1,), (1,)), ((), ())), preferred_element_type=jnp.float32
        ).astype(jnp.bfloat16),
        "space",
        scatter_dimension=0,
        tiled=True,
    )
    temporal = jnp.dot(
        time_factor,
        lax.all_gather(mixed, "space", axis=0, tiled=True),
        preferred_element_type=jnp.float32,
    )
    field = temporal.astype(jnp.bfloat16)
    spill = from_behind(field[: lags - 1], "space", -1)
    extended = jnp.concatenate([field, spill], axis=0)
    offset = lax.axis_index("space") * block_hours
    live_count = tile_count[0, 0]
    starts = tile_hour[:, 0] - offset
    corners = tile_block[:, 0] * width
    live = (jnp.arange(slots, dtype=jnp.int32) < live_count).astype(jnp.float32)
    onehot = (tile_obs[:, 0][:, None] == jnp.arange(observations, dtype=jnp.int32)[None, :]).astype(
        jnp.float32
    )

    def measure(index):
        window = lax.dynamic_slice(extended, (starts[index], corners[index]), (lags, width))
        return jnp.sum(window.astype(jnp.float32) * footprints[index].astype(jnp.float32))

    modeled = jax.vmap(measure)(jnp.arange(slots, dtype=jnp.int32)) * live
    local_totals = jnp.dot(modeled, onehot, precision=lax.Precision.HIGHEST)
    totals = lax.psum(local_totals, ("space", "tm", "obs"))
    innovation = obs_weight * totals
    weights = jnp.dot(onehot, innovation, precision=lax.Precision.HIGHEST) * live

    def deposit(index, grid):
        push = (weights[index] * footprints[index].astype(jnp.float32)).astype(jnp.bfloat16)
        push = lax.optimization_barrier(push).astype(jnp.float32)
        here = lax.dynamic_slice(grid, (starts[index], corners[index]), (lags, width))
        return lax.dynamic_update_slice(grid, here + push, (starts[index], corners[index]))

    blank = jnp.zeros((block_hours + lags - 1, cell_rows), jnp.float32)
    grid = lax.fori_loop(0, slots, deposit, blank)
    tail = from_behind(grid[block_hours:].astype(jnp.bfloat16), "space", 1).astype(jnp.float32)
    arrived = jnp.concatenate(
        [tail, jnp.zeros((block_hours - lags + 1, cell_rows), jnp.float32)], axis=0
    )
    adjoint_field = (grid[:block_hours] + arrived).astype(jnp.bfloat16)
    adjoint_whole = lax.all_gather(adjoint_field, "space", axis=0, tiled=True)
    back_full = lax.dot_general(
        whole_factor, adjoint_whole, (((0,), (0,)), ((), ())), preferred_element_type=jnp.float32
    ).astype(jnp.bfloat16)
    picked = back_full
    spread = lax.psum_scatter(
        jnp.dot(picked, spatial_factor, preferred_element_type=jnp.float32).astype(jnp.bfloat16),
        ("tm", "obs"),
        scatter_dimension=0,
        tiled=True,
    ).astype(jnp.float32)
    return state.astype(jnp.float32) + spread


def solution(mesh):
    return jax.shard_map(
        per_device,
        mesh=mesh,
        in_specs=(
            P(("groups", "tm", "obs"), "space"),
            P(("tm", "obs"), "space"),
            P("space", None),
            P(("groups", "space"), None, ("tm", "obs")),
            P(("groups", "space"), ("tm", "obs")),
            P(("groups", "space"), ("tm", "obs")),
            P(("groups", "space"), ("tm", "obs")),
            P(("groups", "space"), ("tm", "obs")),
            P("groups"),
        ),
        out_specs=P(("groups", "tm", "obs"), "space"),
        check_vma=False,
    )
```

profile of v0, /device:TPU:0, one launch (start us, length us, event | category | flops | bytes accessed | tf_op | source)
XLA Modules:
  0.0 889.4 jit_solution(16792644692123706774)
XLA Ops:
  6.5 0.7 all-gather.5.cloned.1.call-update
  7.3 62.6 %all-gather.5.cloned.1.call-done = bf16[1024,4096]{1,0:T(8,128)(2,1)} async-done(((bf16[256,4096]{1,0:T(8,128)(2,1)}), bf16[1024,4096]{1,0:T(8,128)(2,1)}) %all-gather.5.cloned.1.call-update) | async-done | bytes 8388624 | tf_op jit(solution)/shard_map/all_gather | solution.py:31
  69.9 42.6 %convolution_convert_fusion = bf16[1024,4096]{1,0:T(8,128)(2,1)} fusion(bf16[1024,4096]{1,0:T(8,128)(2,1)} %all-gather.5.cloned.1.call-done, bf16[4096,4096]{1,0:T(8,128)(2,1)} %param.12), kind=kOutput, calls=%fused_computation.12 | convolution fusion | flops 34363932672 | bytes 50331648 | tf_op jit(solution)/shard_map/dot_general | solution.py:34
  112.6 144.6 %reduce-scatter.3.cloned.1.call-done = bf16[256,4096]{1,0:T(8,128)(2,1)} async-done(((bf16[1024,4096]{1,0:T(8,128)(2,1)}), bf16[256,4096]{1,0:T(8,128)(2,1)}) %reduce-scatter.3.cloned.1.call-update) | async-done | bytes 2097168 | tf_op jit(solution)/shard_map/reduce_scatter | solution.py:33
  257.9 151.3 %all-gather.7.cloned.1.call-done = bf16[1024,4096]{1,0:T(8,128)(2,1)} async-done(((bf16[256,4096]{1,0:T(8,128)(2,1)}), bf16[1024,4096]{1,0:T(8,128)(2,1)}) %all-gather.7.cloned.1.call-update) | async-done | bytes 8388624 | tf_op jit(solution)/shard_map/all_gather | solution.py:43
  409.2 5.7 fusion.8
  414.9 1.3 copy-done.1
  416.2 1.3 collective-permute-start
  418.2 0.6 gather_fusion.1
  418.9 0.6 gather_fusion
  420.1 29.0 %collective-permute-done = bf16[47,4096]{1,0:T(8,128)(2,1)} collective-permute-done((bf16[47,4096]{1,0:T(8,128)(2,1)S(1)}, bf16[47,4096]{1,0:T(8,128)(2,1)}, u32[]{:S(2)}, u32[]{:S(2)}) %collective-permute-start) | collective-permute-done | bytes 385056 | tf_op jit(solution)/shard_map/ppermute | solution.py:10
  449.1 1.9 pad_maximum_fusion
  451.0 20.2 %while.15 = (s32[]{:T(128)}, bf16[303,4096]{1,0:T(8,128)(2,1)S(1)}, s32[8,2]{0,1:T(2,128)S(1)}, bf16[8,48,512]{2,1,0:T(8,128)(2,1)}, s32[]{:T(128)}) while((s32[]{:T(128)}, bf16[303,4096]{1,0:T(8,128)(2,1)S(1)}, s32[8,2]{0,1:T(2,128)S(1)}, bf16[8,48,512]{2,1,0:T(8,128)(2,1)}, s32[]{:T(128)}) %tuple.43), condition=%wide.while_cond, body=%wide.while_body.sunk | while | flops 2 | bytes 99437 | solution.py:59
  451.7 1.9 bitcast_dynamic-update-slice_fusion.2
  454.2 1.9 bitcast_dynamic-update-slice_fusion.2
  456.7 1.9 bitcast_dynamic-update-slice_fusion.2
  459.2 1.9 bitcast_dynamic-update-slice_fusion.2
  461.7 1.9 bitcast_dynamic-update-slice_fusion.2
  464.3 1.9 bitcast_dynamic-update-slice_fusion.2
  466.8 1.9 bitcast_dynamic-update-slice_fusion.2
  469.3 1.9 bitcast_dynamic-update-slice_fusion.2
  471.3 1.2 fusion.10
  472.7 29.5 %psum.7 = f32[32]{0:T(128)S(1)} all-reduce(f32[32]{0:T(128)S(1)} %convolution_bitcast_fusion.1), channel_id=1, replica_groups=mesh['groups'=2,'space'=4,'tm'=2,'obs'=2] {'space','tm','obs'}, use_global_device_ids=true, to_apply=%region_2.0 | all-reduce | flops 32 | bytes 256 | tf_op jit(solution)/shard_map/psum | solution.py:64
  502.3 2.8 broadcast_in_dim.2
  505.1 83.1 %while.14 = (s32[]{:T(128)}, f32[303,4096]{1,0:T(8,128)}, s32[8]{0:T(128)S(1)}, s32[8]{0:T(128)S(1)}, f32[8]{0:T(128)S(1)}, /*index=5*/bf16[8,48,512]{2,1,0:T(8,...) while((s32[]{:T(128)}, f32[303,4096]{1,0:T(8,128)}, s32[8]{0:T(128)S(1)}, s32[8]{0:T(128)S(1)}, ...), condition=%wide.region_4.0_spmd, body=%wide.region_3.0_spmd.sunk | while | flops 122888 | bytes 540905 | solution.py:75
  510.2 0.6 dynamic_slice.46
  510.8 0.7 fusion.39
  511.5 1.0 convert_add_fusion.3
  512.5 3.2 dynamic_update_slice.8
  520.7 0.6 dynamic_slice.46
  521.3 0.7 fusion.39
  522.0 1.0 convert_add_fusion.3
  523.0 3.0 dynamic_update_slice.8
  531.0 0.6 dynamic_slice.46
  531.6 0.7 fusion.39
  532.3 1.0 convert_add_fusion.3
  533.3 3.1 dynamic_update_slice.8
  541.5 0.6 dynamic_slice.46
  542.0 0.7 fusion.39
  542.7 1.0 convert_add_fusion.3
  543.7 3.0 dynamic_update_slice.8
  552.4 0.7 fusion.39
  553.1 1.0 convert_add_fusion.3
  554.1 3.1 dynamic_update_slice.8
  562.2 0.6 dynamic_slice.46
  562.8 0.7 fusion.39
  563.5 1.0 convert_add_fusion.3
  564.5 2.9 dynamic_update_slice.8
  573.1 0.7 fusion.39
  573.8 1.0 convert_add_fusion.3
  574.8 3.0 dynamic_update_slice.8
  582.9 0.6 dynamic_slice.46
  583.5 0.7 fusion.39
  584.2 1.0 convert_add_fusion.3
  585.2 3.1 dynamic_update_slice.8
  588.2 1.2 slice.35
  589.4 1.3 collective-permute-start.1
  590.7 6.9 collective-permute-done.1
  597.7 3.8 add_convert_fusion
  601.8 151.2 %all-gather.9.cloned.1.call-done = bf16[1024,4096]{1,0:T(8,128)(2,1)} async-done(((bf16[256,4096]{1,0:T(8,128)(2,1)}), bf16[1024,4096]{1,0:T(8,128)(2,1)}) %all-gather.9.cloned.1.call-update) | async-done | bytes 8388624 | tf_op jit(solution)/shard_map/all_gather | solution.py:81
  753.0 12.9 %fusion.35 = bf16[4096,1024]{1,0:T(8,128)(2,1)S(1)} fusion(bf16[1024,4096]{1,0:T(8,128)(2,1)} %all-gather.9.cloned.1.call-done, bf16[1024,1024]{1,0:T(8,128)(2,1)} %all-gather.11.cloned.1.call-done), kind=kOutput, calls=%fused_computation.9.clone.clone.clone.1 | convolution fusion | flops 8594128896 | bytes 18874368 | tf_op jit(solution)/shard_map/dot_general | solution.py:82
  765.9 42.3 %fusion.5 = bf16[1024,4096]{1,0:T(8,128)(2,1)} fusion(bf16[4096,4096]{1,0:T(8,128)(2,1)} %param.12, bf16[4096,1024]{1,0:T(8,128)(2,1)S(1)} %fusion.35), kind=kOutput, calls=%fused_computation.11 | convolution fusion | flops 34363932672 | bytes 50331648 | tf_op jit(solution)/shard_map/dot_general | solution.py:87
  808.2 70.1 %reduce-scatter.5.cloned.1.call-done = bf16[256,4096]{1,0:T(8,128)(2,1)} async-done(((bf16[1024,4096]{1,0:T(8,128)(2,1)}), bf16[256,4096]{1,0:T(8,128)(2,1)}) %reduce-scatter.5.cloned.1.call-update) | async-done | bytes 2097168 | tf_op jit(solution)/shard_map/reduce_scatter | solution.py:86
  878.3 4.3 convert_add_fusion.1
  (73 shorter events, 17.3 us)
Async XLA Ops:
  6.5 63.4 %all-gather.5.cloned.1.call-start = ((), (), s32[]{:S(2)}) async-start(), calls=%async_computation.2 | async-start | bytes 10485760 | tf_op jit(solution)/shard_map/all_gather | solution.py:31
  7.3 249.9 %reduce-scatter.3.cloned.1.call-start = ((), (), s32[]{:S(2)}) async-start(), calls=%async_computation.3 | async-start | bytes 10485760 | tf_op jit(solution)/shard_map/reduce_scatter | solution.py:33
  112.5 145.3 %copy-start.4 = (s32[8,1]{0,1:T(1,128)S(1)}, s32[8,1]{0,1:T(1,128)}, u32[]{:S(2)}) copy-start(s32[8,1]{0,1:T(1,128)} %param.16) | copy-start | bytes 100
  112.5 145.3 %copy-start.5 = (s32[8,1]{0,1:T(1,128)S(1)}, s32[8,1]{0,1:T(1,128)}, u32[]{:S(2)}) copy-start(s32[8,1]{0,1:T(1,128)} %param.17) | copy-start | bytes 100
  112.5 296.6 %copy-start.3 = (bf16[256,1024]{1,0:T(8,128)(2,1)S(1)}, bf16[256,1024]{1,0:T(8,128)(2,1)}, u32[]{:S(2)}) copy-start(bf16[256,1024]{1,0:T(8,128)(2,1)} %param.13) | copy-start | bytes 1572868
  112.5 296.6 %all-gather.7.cloned.1.call-start = ((), (), s32[]{:S(2)}) async-start(), calls=%async_computation.4 | async-start | bytes 10485760 | tf_op jit(solution)/shard_map/all_gather | solution.py:43
  257.2 344.6 %all-gather.11.cloned.1.call-start = ((), (), s32[]{:S(2)}) async-start(), calls=%async_computation.6 | async-start | bytes 2621440 | tf_op jit(solution)/shard_map/all_gather | solution.py:30
  257.8 495.2 %all-gather.9.cloned.1.call-start = ((), (), s32[]{:S(2)}) async-start(), calls=%async_computation.5 | async-start | bytes 10485760 | tf_op jit(solution)/shard_map/all_gather | solution.py:81
  257.9 161.6 %copy-start.2 = (bf16[8,48,512]{2,1,0:T(8,128)(2,1)S(1)}, bf16[8,48,512]{2,1,0:T(8,128)(2,1)}, u32[]{:S(2)}) copy-start(bf16[8,48,512]{2,1,0:T(8,128)(2,1)} %param.14) | copy-start | bytes 1179652
  414.9 1.3 copy-start.1
  416.2 56.3 %copy-start.6 = (s32[8,1]{0,1:T(1,128)S(1)}, s32[8,1]{0,1:T(1,128)}, u32[]{:S(2)}) copy-start(s32[8,1]{0,1:T(1,128)} %param.15) | copy-start | bytes 100
  416.2 85.9 %copy-start.7 = (f32[32]{0:T(128)S(1)}, f32[32]{0:T(128)}, u32[]{:S(2)}) copy-start(f32[32]{0:T(128)} %param.19) | copy-start | bytes 388
  416.2 32.9 %collective-permute-start = (bf16[47,4096]{1,0:T(8,128)(2,1)S(1)}, bf16[47,4096]{1,0:T(8,128)(2,1)}, u32[]{:S(2)}, u32[]{:S(2)}) collective-permute-start(bf16[47,4096]{1,0:T(8,128)(2,1)S(1)} %slice.31), channel_id=1, source_target_pairs={{4,0},{8,4},{12,8},{5,1},{9,5},{13,9},{6,2},{10,6},{14,10},{7,3},{... | collective-permute-start | bytes 1155080 | tf_op jit(solution)/shard_map/ppermute | solution.py:10
  589.4 8.3 collective-permute-start.1
  601.5 276.8 %reduce-scatter.5.cloned.1.call-start = ((), (), s32[]{:S(2)}) async-start(), calls=%async_computation.7 | async-start | bytes 10485760 | tf_op jit(solution)/shard_map/reduce_scatter | solution.py:86
  808.2 70.1 %copy-start = (bf16[256,4096]{1,0:T(8,128)(2,1)S(1)}, bf16[256,4096]{1,0:T(8,128)(2,1)}, u32[]{:S(2)}) copy-start(bf16[256,4096]{1,0:T(8,128)(2,1)} %param.11) | copy-start | bytes 6291460
Sparse Core Ops, SparseCore 0:
  8.9 60.9 all-gather.4
  112.7 144.4 reduce-scatter.2
  258.7 150.3 all-gather.6
  410.6 51.5 all-gather.10
  601.6 151.2 all-gather.8
  808.3 69.9 reduce-scatter.4
where the time goes:
time: 891 us; the launch traced here: 889 us
  waiting for transfers between devices  617 us (69%)
  matrix products  104 us (12%)
  local copies, waits for them, and re-layouts  65.9 us (7%)
  loops' own time  31.3 us (4%)
  blocking collectives  29.5 us (3%)
  other arithmetic  24.7 us (3%)
  between operations  14.3 us (2%)
    all_gather x1, waiting for transfers between devices, per_device(): lax.all_gather(mixed, 'space', axis=0, tiled=True)  151 us
    all_gather x1, waiting for transfers between devices, per_device(): adjoint_whole = lax.all_gather(adjoint_field, 'space', axis=0, tiled=True)  151 us
    reduce_scatter x1, waiting for transfers between devices, per_device(): lax.psum_scatter(lax.dot_general(picked, spatial_factor, (((1,), (1,)), (...  145 us
    reduce_scatter x1, waiting for transfers between devices, per_device(): lax.psum_scatter(jnp.dot(picked, spatial_factor, preferred_element_type=j...  70.1 us
    all_gather x1, waiting for transfers between devices, per_device(): full_state = lax.all_gather(state, ('tm', 'obs'), axis=0, tiled=True)  62.6 us
    dot_general x1, matrix products, per_device(): lax.dot_general(picked, spatial_factor, (((1,), (1,)), ((), ())), preferr...  42.6 us
    dot_general x1, matrix products, per_device(): jnp.dot(picked, spatial_factor, preferred_element_type=jnp.float32)  42.3 us
    ppermute x2, waiting for transfers between devices, from_behind(): lax.ppermute(value, axis, [(source, source + steps) for source in range(l...  35.9 us
  transfers between devices with their start and end apart: 8, of which 7 were waited for; matrix products, arithmetic and copies ran while one was open for 10% of the time, Pallas kernels for 0%

commit v1 on v0

v1 whole, which is shorter than its diff:
```python
import functools

import jax
import jax.numpy as jnp
from jax import lax
from jax.experimental import pallas as pl
from jax.experimental.pallas import tpu as pltpu
from jax.sharding import PartitionSpec as P

ALIGN = 16
GROUP = 4


def chunk_of(columns, most):
    chunk = min(columns, most)
    while columns % chunk:
        chunk //= 2
    return chunk


def image_kernel(lags, rows, step, order_ref, shift_ref, start_ref, tiles_ref, factor_ref, image_ref, held):
    block = pl.program_id(0)
    begin, end = start_ref[block], start_ref[block + 1]
    last = order_ref.shape[0] - 1
    width = tiles_ref.shape[2]
    columns = factor_ref.shape[1]

    def group(index, carry):
        first = begin + index * GROUP
        for k in range(GROUP):
            at = jnp.minimum(first + k, last)
            tile = tiles_ref[order_ref[at]].astype(jnp.float32)
            tile = jnp.concatenate([tile, jnp.zeros((rows - lags, width), jnp.float32)], axis=0)
            tile = pltpu.roll(tile, shift_ref[at], 0)
            held[k * rows : (k + 1) * rows, :] = tile.astype(jnp.bfloat16)

        def part(piece, inner):
            span = pl.ds(pl.multiple_of(piece * step, step), step)
            product = jnp.dot(held[...], factor_ref[:, span], preferred_element_type=jnp.float32)
            product = product.astype(jnp.bfloat16)
            for k in range(GROUP):

                @pl.when(first + k < end)
                def _():
                    image_ref[first + k, :, span] = product[k * rows : (k + 1) * rows]

            return inner

        lax.fori_loop(0, columns // step, part, 0)
        return carry

    lax.fori_loop(0, (end - begin + GROUP - 1) // GROUP, group, 0)


def images(order, shift, start, tiles, factor, rows):
    count, lags, width = tiles.shape
    cells, columns = factor.shape
    step = chunk_of(columns, 1024)
    return pl.pallas_call(
        functools.partial(image_kernel, lags, rows, step),
        grid_spec=pltpu.PrefetchScalarGridSpec(
            num_scalar_prefetch=3,
            grid=(cells // width,),
            in_specs=[
                pl.BlockSpec((count, lags, width), lambda i, *_: (0, 0, 0)),
                pl.BlockSpec((width, columns), lambda i, *_: (i, 0)),
            ],
            out_specs=pl.BlockSpec((count, rows, columns), lambda i, *_: (0, 0, 0)),
            scratch_shapes=[pltpu.VMEM((GROUP * rows, width), jnp.bfloat16)],
        ),
        out_shape=jax.ShapeDtypeStruct((count, rows, columns), jnp.bfloat16),
        compiler_params=pltpu.CompilerParams(vmem_limit_bytes=58 * 1024 * 1024),
        cost_estimate=pl.CostEstimate(
            flops=2 * count * rows * width * columns, bytes_accessed=2 * cells * columns, transcendentals=0
        ),
        name="images",
    )(order, shift, start, tiles, factor)


def window_kernel(rows, base_ref, live_ref, factor_ref, state_ref, image_ref, sums_ref, field):
    @pl.when(pl.program_id(0) == 0)
    def _():
        sums_ref[...] = jnp.zeros_like(sums_ref)

    field[...] = jnp.dot(factor_ref[...], state_ref[...], preferred_element_type=jnp.float32)
    columns = state_ref.shape[1]

    def one(at, carry):
        base = pl.multiple_of(base_ref[at], ALIGN)
        product = field[pl.ds(base, rows), :] * image_ref[at].astype(jnp.float32)
        product = jnp.sum(product.reshape(rows // 8, 8, columns), axis=0)
        total = product[:, :128]
        for k in range(1, columns // 128):
            total = total + product[:, k * 128 : (k + 1) * 128]
        sums_ref[at] += total
        return carry

    lax.fori_loop(0, live_ref[0], one, 0)


def window_sums(base, live, factor, state, image):
    hours, columns = state.shape
    count, rows, _ = image.shape
    step = chunk_of(columns, 512)
    return pl.pallas_call(
        functools.partial(window_kernel, rows),
        grid_spec=pltpu.PrefetchScalarGridSpec(
            num_scalar_prefetch=2,
            grid=(columns // step,),
            in_specs=[
                pl.BlockSpec((hours, hours), lambda i, *_: (0, 0)),
                pl.BlockSpec((hours, step), lambda i, *_: (0, i)),
                pl.BlockSpec((count, rows, step), lambda i, *_: (0, 0, i)),
            ],
            out_specs=pl.BlockSpec((count, 8, 128), lambda i, *_: (0, 0, 0)),
            scratch_shapes=[pltpu.VMEM((hours, step), jnp.float32)],
        ),
        out_shape=jax.ShapeDtypeStruct((count, 8, 128), jnp.float32),
        compiler_params=pltpu.CompilerParams(vmem_limit_bytes=58 * 1024 * 1024),
        name="window_sums",
    )(base, live, factor, state, image)


def back_kernel(rows, base_ref, live_ref, weight_ref, factor_ref, image_ref, out_ref, grid):
    grid[...] = jnp.zeros_like(grid)

    def one(at, carry):
        window = pl.ds(pl.multiple_of(base_ref[at], ALIGN), rows)
        grid[window, :] += weight_ref[at] * image_ref[at].astype(jnp.float32)
        return carry

    lax.fori_loop(0, live_ref[0], one, 0)
    out_ref[...] = lax.dot_general(
        factor_ref[...],
        grid[...].astype(jnp.bfloat16),
        (((1,), (0,)), ((), ())),
        preferred_element_type=jnp.float32,
    ).astype(jnp.bfloat16)


def back_product(base, live, weight, factor, image):
    hours = factor.shape[0]
    count, rows, columns = image.shape
    step = chunk_of(columns, 512)
    return pl.pallas_call(
        functools.partial(back_kernel, rows),
        grid_spec=pltpu.PrefetchScalarGridSpec(
            num_scalar_prefetch=3,
            grid=(columns // step,),
            in_specs=[
                pl.BlockSpec((hours, hours), lambda i, *_: (0, 0)),
                pl.BlockSpec((count, rows, step), lambda i, *_: (0, 0, i)),
            ],
            out_specs=pl.BlockSpec((hours, step), lambda i, *_: (0, i)),
            scratch_shapes=[pltpu.VMEM((hours, step), jnp.float32)],
        ),
        out_shape=jax.ShapeDtypeStruct((hours, columns), jnp.bfloat16),
        compiler_params=pltpu.CompilerParams(vmem_limit_bytes=58 * 1024 * 1024),
        name="back_product",
    )(base, live, weight, factor, image)


def per_device(
    state,
    spatial_factor,
    time_factor,
    footprints,
    tile_obs,
    tile_block,
    tile_hour,
    tile_count,
    obs_weight,
):
    slots, lags, width = footprints.shape
    blocks = spatial_factor.shape[0] // width
    observations = obs_weight.shape[0]
    rows = -(-lags // ALIGN) * ALIGN + ALIGN
    own_live = (jnp.arange(slots, dtype=jnp.int32)[:, None] < tile_count).astype(jnp.int32)
    table = lax.all_gather(
        jnp.concatenate([tile_obs, tile_block, tile_hour, own_live], axis=1), "space", axis=0, tiled=True
    )
    tiles = lax.all_gather(footprints, "space", axis=0, tiled=True)
    factor = lax.all_gather(time_factor, "space", axis=0, tiled=True)
    full_state = lax.all_gather(state, ("tm", "obs"), axis=0, tiled=True)
    hours = factor.shape[0]
    count = tiles.shape[0]

    key = jnp.where(table[:, 3] > 0, table[:, 1], blocks)
    number = jnp.arange(count, dtype=jnp.int32)
    before = (key[None, :] < key[:, None]) | ((key[None, :] == key[:, None]) & (number[None, :] < number[:, None]))
    rank = jnp.sum(before.astype(jnp.int32), axis=1)
    at_rank = (rank[None, :] == number[:, None]).astype(jnp.int32)
    order = jnp.sum(at_rank * number[None, :], axis=1)
    hour = jnp.sum(at_rank * table[:, 2][None, :], axis=1)
    obs = jnp.sum(at_rank * table[:, 0][None, :], axis=1)
    edges = jnp.arange(blocks + 1, dtype=jnp.int32)
    start = jnp.sum((key[None, :] < edges[:, None]).astype(jnp.int32), axis=1)
    live = start[blocks:]
    base = jnp.minimum(hour // ALIGN * ALIGN, hours - rows)
    shift = hour - base

    image = images(order, shift, start, tiles, spatial_factor, rows)
    sums = window_sums(base, live, factor, full_state, image)
    modeled = jnp.where(number < live, jnp.sum(sums, axis=(1, 2)), 0.0)
    onehot = obs[:, None] == jnp.arange(observations, dtype=jnp.int32)[None, :]
    local_totals = jnp.sum(jnp.where(onehot, modeled[:, None], 0.0), axis=0)
    innovation = obs_weight * lax.psum(local_totals, ("space", "tm", "obs"))
    weight = jnp.sum(jnp.where(onehot, innovation[None, :], 0.0), axis=1)
    spread = lax.psum_scatter(
        back_product(base, live, weight, factor, image), ("tm", "obs"), scatter_dimension=0, tiled=True
    )
    return state.astype(jnp.float32) + spread.astype(jnp.float32)


def solution(mesh):
    return jax.shard_map(
        per_device,
        mesh=mesh,
        in_specs=(
            P(("groups", "tm", "obs"), "space"),
            P(("tm", "obs"), "space"),
            P("space", None),
            P(("groups", "space"), None, ("tm", "obs")),
            P(("groups", "space"), ("tm", "obs")),
            P(("groups", "space"), ("tm", "obs")),
            P(("groups", "space"), ("tm", "obs")),
            P(("groups", "space"), ("tm", "obs")),
            P("groups"),
        ),
        out_specs=P(("groups", "tm", "obs"), "space"),
        check_vma=False,
    )
```

time: 891 us -> 307 us (0.34)
  waiting for transfers between devices: 617 us -> 173 us
  matrix products: 104 us -> 0 us
  local copies, waits for them, and re-layouts: 65.9 us -> 0.75 us
  Pallas kernels: 0 us -> 64.1 us
  loops' own time: 31.3 us -> 0 us
  blocking collectives: 29.5 us -> 46 us
  other arithmetic: 24.7 us -> 9.2 us
    all_gather x3 -> x2, waiting for transfers between devices: 302 us -> 42.8 us  [the longest x1 22.7 us: per_device(): tiles = lax.all_gather(footprints, 'space', axis=0, tiled=True)]
    reduce_scatter x2 -> x1, waiting for transfers between devices: 215 us -> 69.2 us  [per_device(): lax.psum_scatter(back_product(base, live, weight, factor, image), ('tm',...]
    dot_general x6 -> x0, matrix products: 104 us -> none  [the longest x1 42.6 us: per_device(): lax.dot_general(picked, spatial_factor, (((1,), (1,)), ((), ())), preferr...]
    pallas_call x0 -> x3, Pallas kernels: none -> 64.1 us  [the longest x1 26.3 us: images(): pl.pallas_call(functools.partial(image_kernel, lags, rows, step), grid_sp...]
    ppermute x2 -> x0, waiting for transfers between devices: 35.9 us -> none  [from_behind(): lax.ppermute(value, axis, [(source, source + steps) for source in range(l...]
    another operation x2 -> x0, loops' own time: 31.3 us -> none  [the longest x1 31.2 us: per_device(): grid = lax.fori_loop(0, slots, deposit, blank)]
    dynamic_update_slice x8 -> x0, local copies, waits for them, and re-layouts: 24.4 us -> none  [deposit(): lax.dynamic_update_slice(grid, here + push, (starts[index], corners[index]))]
    gather x27 -> x0, local copies, waits for them, and re-layouts: 22.1 us -> none
  transfers between devices with their start and end apart: 8 -> 4, of which waited for: 7 -> 4; matrix products, arithmetic and copies ran while one was open for 10% -> 1% of each run, Pallas kernels for 0% -> 9%
where the time goes in v1:
time: 307 us
  waiting for transfers between devices  173 us (56%)
  Pallas kernels  64.1 us (21%)
  blocking collectives  46 us (15%)
  between operations  13.8 us (4%)
  other arithmetic  9.2 us (3%)
    reduce_scatter x1, waiting for transfers between devices, per_device(): lax.psum_scatter(back_product(base, live, weight, factor, image), ('tm',...  69.2 us
    all_gather x1, waiting for transfers between devices, per_device(): full_state = lax.all_gather(state, ('tm', 'obs'), axis=0, tiled=True)  58.6 us
    psum x1, blocking collectives, per_device(): innovation = obs_weight * lax.psum(local_totals, ('space', 'tm', 'obs'))  32.3 us
    pallas_call x1, Pallas kernels, images(): pl.pallas_call(functools.partial(image_kernel, lags, rows, step), grid_sp...  26.3 us
    all_gather x1, waiting for transfers between devices, per_device(): tiles = lax.all_gather(footprints, 'space', axis=0, tiled=True)  22.7 us
    all_gather x1, waiting for transfers between devices, per_device(): factor = lax.all_gather(time_factor, 'space', axis=0, tiled=True)  20.1 us
    pallas_call x1, Pallas kernels, back_product(): pl.pallas_call(functools.partial(back_kernel, rows), grid_spec=pltpu.Pref...  19.2 us
    pallas_call x1, Pallas kernels, window_sums(): pl.pallas_call(functools.partial(window_kernel, rows), grid_spec=pltpu.Pr...  18.6 us
  transfers between devices with their start and end apart: 4, of which 4 were waited for; matrix products, arithmetic and copies ran while one was open for 1% of the time, Pallas kernels for 9%

profile of v1, /device:TPU:0, one launch (start us, length us, event | category | flops | bytes accessed | tf_op | source)
XLA Modules:
  0.0 306.6 jit_solution(15855139119046929440)
XLA Ops:
  6.5 0.0 all-gather.9.cloned.1.call-start
  6.5 0.7 all-gather.9.cloned.1.call-update
  7.3 0.0 all-gather.5.cloned.1.call-start
  7.3 0.7 all-gather.5.cloned.1.call-update
  8.0 0.0 all-gather.7.cloned.1.call-start
  8.1 0.7 all-gather.7.cloned.1.call-update
  8.7 0.0 reduce-scatter.2.cloned.1.call-start
  9.4 0.7 add_bitcast_fusion
  10.1 13.6 %all-gather = s32[4,8,4]{1,2,0:T(4,128)S(1)} all-gather(s32[1,8,4]{1,2,0:T(4,128)S(1)} %add_bitcast_fusion), channel_id=1, replica_groups=mesh['groups'=2,'space'=4,'tm'=2,'obs'=2] {'space'}, dimensions={0}, use_global_device_ids=true | all-gather | bytes 640 | tf_op jit(solution)/shard_map/all_gather | solution.py:179
  23.8 0.1 reshape.41
  23.9 0.1 convert_reduce_fusion.1.start_ref
  24.0 0.0 copy-start.1
  24.0 0.6 slice.18.live_ref
  24.7 0.2 convert_reduce_fusion
  24.8 0.6 select_reduce_fusion.3
  25.5 0.6 fusion.3
  26.1 22.7 %all-gather.9.cloned.1.call-done.tiles_ref = bf16[32,48,512]{2,1,0:T(8,128)(2,1)} async-done(((bf16[8,48,512]{2,1,0:T(8,128)(2,1)}), bf16[32,48,512]{2,1,0:T(8,128)(2,1)}) %all-gather.9.cloned.1.call-update) | async-done | bytes 1572880 | tf_op jit(solution)/shard_map/all_gather | solution.py:182
  48.8 0.0 copy-done.1
  48.8 26.3 %images.1.image_ref = bf16[32,64,4096]{2,1,0:T(8,128)(2,1)} custom-call(s32[32]{0:T(128)} %get-tuple-element.6.order_ref, s32[32]{0:T(128)} %get-tuple-element.8.shift_ref, s32[9]{0:T(128)} %copy-done.1, bf16[32,48,512]{2,1,0:T(8,128)(2,1)} %all-gather.9.cloned.1.call-done.tiles_ref, bf16[4096,4096]{1,0:T(8,128)(2,1)} %factor_ref.1), custom_call_target="tpu_custom_call" | custom-call | flops 8589934592 | bytes 33554432 | tf_op jit(solution)/shard_map/images/pallas_call | solution.py:59
  75.0 20.1 %all-gather.5.cloned.1.call-done.factor_ref = bf16[1024,1024]{1,0:T(8,128)(2,1)} async-done(((bf16[256,1024]{1,0:T(8,128)(2,1)}), bf16[1024,1024]{1,0:T(8,128)(2,1)}) %all-gather.5.cloned.1.call-update) | async-done | bytes 2097168 | tf_op jit(solution)/shard_map/all_gather | solution.py:183
  95.2 58.6 %all-gather.7.cloned.1.call-done.state_ref = bf16[1024,4096]{1,0:T(8,128)(2,1)} async-done(((bf16[256,4096]{1,0:T(8,128)(2,1)}), bf16[1024,4096]{1,0:T(8,128)(2,1)}) %all-gather.7.cloned.1.call-update) | async-done | bytes 8388624 | tf_op jit(solution)/shard_map/all_gather | solution.py:184
  153.7 0.0 copy-start.2
  153.8 18.6 %window_sums.1 = f32[32,8,128]{2,1,0:T(8,128)} custom-call(s32[32]{0:T(128)} %get-tuple-element.9.base_ref, s32[1]{0:T(128)} %slice.18.live_ref, bf16[1024,1024]{1,0:T(8,128)(2,1)} %all-gather.5.cloned.1.call-done.factor_ref, bf16[1024,4096]{1,0:T(8,128)(2,1)} %all-gather.7.cloned.1.call-done.state_ref, bf16[32,64,4096]{2,1,0:T(8,128)(2,1)} %images.1.image_ref), custom_call_target="tpu_custom_call" | custom-call | tf_op jit(solution)/shard_map/window_sums/pallas_call | solution.py:105
  172.3 1.2 reduce_sum.77
  173.5 0.6 compare_select_fusion
  174.2 0.1 select_reduce_fusion.1
  174.3 32.3 %psum.7 = f32[32]{0:T(128)S(1)} all-reduce(f32[32]{0:T(128)S(1)} %select_reduce_fusion.1), channel_id=1, replica_groups=mesh['groups'=2,'space'=4,'tm'=2,'obs'=2] {'space','tm','obs'}, use_global_device_ids=true, to_apply=%region_7.8 | all-reduce | flops 32 | bytes 256 | tf_op jit(solution)/shard_map/psum | solution.py:207
  206.6 0.0 copy-done.2
  206.6 0.7 select_reduce_fusion.weight_ref
  207.3 19.2 %back_product.1 = bf16[1024,4096]{1,0:T(8,128)(2,1)} custom-call(s32[32]{0:T(128)} %get-tuple-element.9.base_ref, s32[1]{0:T(128)} %slice.18.live_ref, f32[32]{0:T(128)} %select_reduce_fusion.weight_ref, bf16[1024,1024]{1,0:T(8,128)(2,1)} %all-gather.5.cloned.1.call-done.factor_ref, bf16[32,64,4096]{2,1,0:T(8,128)(2,1)} %images.1.image_ref), custom_call_target="tpu_custom_call" | custom-call | tf_op jit(solution)/shard_map/back_product/pallas_call | solution.py:145
  226.6 0.0 copy-start
  226.6 0.0 reduce-scatter.2.cloned.1.call-update
  226.6 69.2 %reduce-scatter.2.cloned.1.call-done = bf16[256,4096]{1,0:T(8,128)(2,1)} async-done(((bf16[1024,4096]{1,0:T(8,128)(2,1)}), bf16[256,4096]{1,0:T(8,128)(2,1)}) %reduce-scatter.2.cloned.1.call-update) | async-done | bytes 2097168 | tf_op jit(solution)/shard_map/reduce_scatter | solution.py:209
  295.7 0.0 copy-done
  295.7 4.3 %convert_add_fusion = f32[256,4096]{1,0:T(8,128)} fusion(bf16[256,4096]{1,0:T(8,128)(2,1)} %reduce-scatter.2.cloned.1.call-done, bf16[256,4096]{1,0:T(8,128)(2,1)S(1)} %copy-done), kind=kLoop, calls=%fused_computation | loop fusion | flops 3145728 | bytes 8388608 | tf_op jit(solution)/shard_map/add | solution.py:212
  (4 shorter events, 0.0 us)
Async XLA Ops:
  6.5 42.2 %all-gather.9.cloned.1.call-start = ((), (), s32[]{:S(2)}) async-start(), calls=%async_computation.3 | async-start | bytes 1966080 | tf_op jit(solution)/shard_map/all_gather | solution.py:182
  7.3 87.9 %all-gather.5.cloned.1.call-start = ((), (), s32[]{:S(2)}) async-start(), calls=%async_computation.1 | async-start | bytes 2621440 | tf_op jit(solution)/shard_map/all_gather | solution.py:183
  8.0 145.7 %all-gather.7.cloned.1.call-start = ((), (), s32[]{:S(2)}) async-start(), calls=%async_computation.2 | async-start | bytes 10485760 | tf_op jit(solution)/shard_map/all_gather | solution.py:184
  8.7 287.0 %reduce-scatter.2.cloned.1.call-start = ((), (), s32[]{:S(2)}) async-start(), calls=%async_computation.4 | async-start | bytes 10485760 | tf_op jit(solution)/shard_map/reduce_scatter | solution.py:209
  24.0 24.8 %copy-start.1 = (s32[9]{0:T(128)}, s32[9]{0:T(128)S(1)}, u32[]{:S(2)}) copy-start(s32[9]{0:T(128)S(1)} %convert_reduce_fusion.1.start_ref) | copy-start | bytes 112
  153.7 52.9 %copy-start.2 = (f32[32]{0:T(128)S(1)}, f32[32]{0:T(128)}, u32[]{:S(2)}) copy-start(f32[32]{0:T(128)} %param.17) | copy-start | bytes 388
  226.6 69.2 %copy-start = (bf16[256,4096]{1,0:T(8,128)(2,1)S(1)}, bf16[256,4096]{1,0:T(8,128)(2,1)}, u32[]{:S(2)}) copy-start(bf16[256,4096]{1,0:T(8,128)(2,1)} %param.9) | copy-start | bytes 6291460
Sparse Core Ops, SparseCore 0:
  8.9 39.8 all-gather.8
  50.3 44.7 all-gather.4
  96.7 56.9 all-gather.6
  226.7 68.9 reduce-scatter.1

commit v2 on v1

--- a/solution.py
+++ b/solution.py
@@ -9,6 +9,7 @@
 
 ALIGN = 16
 GROUP = 4
+MESH = pl.DeviceIdType.MESH
 
 
 def chunk_of(columns, most):
@@ -121,7 +122,7 @@
     )(base, live, factor, state, image)
 
 
-def back_kernel(rows, base_ref, live_ref, weight_ref, factor_ref, image_ref, out_ref, grid):
+def place_kernel(rows, base_ref, live_ref, weight_ref, image_ref, out_ref, grid):
     grid[...] = jnp.zeros_like(grid)
 
     def one(at, carry):
@@ -130,34 +131,367 @@
         return carry
 
     lax.fori_loop(0, live_ref[0], one, 0)
-    out_ref[...] = lax.dot_general(
-        factor_ref[...],
-        grid[...].astype(jnp.bfloat16),
-        (((1,), (0,)), ((), ())),
-        preferred_element_type=jnp.float32,
-    ).astype(jnp.bfloat16)
-
-
-def back_product(base, live, weight, factor, image):
-    hours = factor.shape[0]
+    out_ref[...] = grid[...].astype(jnp.bfloat16)
+
+
+def placed(base, live, weight, image, hours):
     count, rows, columns = image.shape
     step = chunk_of(columns, 512)
     return pl.pallas_call(
-        functools.partial(back_kernel, rows),
+        functools.partial(place_kernel, rows),
         grid_spec=pltpu.PrefetchScalarGridSpec(
             num_scalar_prefetch=3,
             grid=(columns // step,),
-            in_specs=[
-                pl.BlockSpec((hours, hours), lambda i, *_: (0, 0)),
-                pl.BlockSpec((count, rows, step), lambda i, *_: (0, 0, i)),
-            ],
+            in_specs=[pl.BlockSpec((count, rows, step), lambda i, *_: (0, 0, i))],
             out_specs=pl.BlockSpec((hours, step), lambda i, *_: (0, i)),
             scratch_shapes=[pltpu.VMEM((hours, step), jnp.float32)],
         ),
         out_shape=jax.ShapeDtypeStruct((hours, columns), jnp.bfloat16),
         compiler_params=pltpu.CompilerParams(vmem_limit_bytes=58 * 1024 * 1024),
-        name="back_product",
-    )(base, live, weight, factor, image)
+        name="placed",
+    )(base, live, weight, image)
+
+
+def gather_kernel(
+    n,
+    m,
+    tiles_ref,
+    factor_ref,
+    table_ref,
+    tiles_out,
+    factor_out,
+    table_out,
+    own_sem,
+    table_send,
+    table_recv,
+    tile_send,
+    tile_recv,
+    part_send,
+    part_recv,
+    core_send,
+    core_recv,
+):
+    me, core = lax.axis_index("space"), lax.axis_index("obs")
+    slots, block = tiles_ref.shape[0], factor_ref.shape[0]
+    part = block // m
+    barrier = pltpu.get_barrier_semaphore()
+    ways = (1, -1)
+
+    def inside(index):
+        return (index >= 0) & (index < n)
+
+    for way in ways:
+
+        @pl.when(inside(me + way))
+        def _():
+            pl.semaphore_signal(barrier, inc=1, device_id={"space": me + way}, device_id_type=MESH)
+
+    for other in range(1, m):
+        pl.semaphore_signal(barrier, inc=1, device_id={"obs": lax.rem(core + other, m)}, device_id_type=MESH)
+    ends = jnp.where(me > 0, 1, 0) + jnp.where(me < n - 1, 1, 0)
+    pl.semaphore_wait(barrier, ends + (m - 1))
+
+    def tile_rows(index):
+        return tiles_out.at[pl.ds(index * slots, slots)]
+
+    def part_rows(index, which):
+        start = pl.multiple_of(index * block + which * part, part)
+        return factor_out.at[pl.ds(start, part)]
+
+    own_tiles = pltpu.make_async_copy(tiles_ref, tile_rows(me), own_sem.at[0])
+    own_factor = pltpu.make_async_copy(
+        factor_ref, factor_out.at[pl.ds(pl.multiple_of(me * block, block), block)], own_sem.at[1]
+    )
+    own_table = pltpu.make_async_copy(table_ref, table_out.at[me], own_sem.at[2])
+    own_table.start()
+    own_tiles.start()
+    own_factor.start()
+
+    def table_copy(d, k, index, first):
+        return pltpu.make_async_remote_copy(
+            src_ref=table_ref if first else table_out.at[index],
+            dst_ref=table_out.at[index],
+            send_sem=table_send.at[d, k],
+            recv_sem=table_recv.at[d, k],
+            device_id={"space": me + ways[d]},
+            device_id_type=MESH,
+        )
+
+    def tile_copy(d, k, index, first):
+        return pltpu.make_async_remote_copy(
+            src_ref=tiles_ref if first else tile_rows(index),
+            dst_ref=tile_rows(index),
+            send_sem=tile_send.at[d, k],
+            recv_sem=tile_recv.at[d, k],
+            device_id={"space": me + ways[d]},
+            device_id_type=MESH,
+        )
+
+    def part_copy(d, k, index, first):
+        source = factor_ref.at[pl.ds(pl.multiple_of(core * part, part), part)] if first else part_rows(index, core)
+        return pltpu.make_async_remote_copy(
+            src_ref=source,
+            dst_ref=part_rows(index, core),
+            send_sem=part_send.at[d, k],
+            recv_sem=part_recv.at[d, k],
+            device_id={"space": me + ways[d]},
+            device_id_type=MESH,
+        )
+
+    def core_copy(d, k, other, index, which):
+        return pltpu.make_async_remote_copy(
+            src_ref=part_rows(index, which),
+            dst_ref=part_rows(index, which),
+            send_sem=core_send.at[other - 1, d, k],
+            recv_sem=core_recv.at[other - 1, d, k],
+            device_id={"obs": lax.rem(core + other, m)},
+            device_id_type=MESH,
+        )
+
+    for k in range(n):
+        for d, way in enumerate(ways):
+            if k > 0:
+
+                @pl.when(inside(me - way * k))
+                def _():
+                    table_copy(d, k - 1, me - way * k, False).wait_recv()
+                    tile_copy(d, k - 1, me - way * k, False).wait_recv()
+
+            if k < n - 1:
+
+                @pl.when(inside(me - way * k) & inside(me + way))
+                def _():
+                    table_copy(d, k, me - way * k, k == 0).start()
+                    tile_copy(d, k, me - way * k, k == 0).start()
+
+        for d, way in enumerate(ways):
+            if k > 0:
+
+                @pl.when(inside(me - way * k))
+                def _():
+                    part_copy(d, k - 1, me - way * k, False).wait_recv()
+
+            if k < n - 1:
+
+                @pl.when(inside(me - way * k) & inside(me + way))
+                def _():
+                    part_copy(d, k, me - way * k, k == 0).start()
+
+            if k > 0:
+
+                @pl.when(inside(me - way * k))
+                def _():
+                    for other in range(1, m):
+                        core_copy(d, k - 1, other, me - way * k, core).start()
+
+    for k in range(1, n):
+        for d, way in enumerate(ways):
+
+            @pl.when(inside(me - way * k))
+            def _():
+                for other in range(1, m):
+                    came = core_copy(d, k - 1, other, me - way * k, lax.rem(core + m - other, m))
+                    came.wait_recv()
+                    core_copy(d, k - 1, other, me - way * k, core).wait_send()
+
+    for k in range(n - 1):
+        for d, way in enumerate(ways):
+
+            @pl.when(inside(me - way * k) & inside(me + way))
+            def _():
+                table_copy(d, k, me - way * k, k == 0).wait_send()
+                tile_copy(d, k, me - way * k, k == 0).wait_send()
+                part_copy(d, k, me - way * k, k == 0).wait_send()
+
+    own_table.wait()
+    own_tiles.wait()
+    own_factor.wait()
+
+
+def gathered(footprints, time_factor, table):
+    n, m = lax.axis_size("space"), lax.axis_size("obs")
+    slots, lags, width = footprints.shape
+    block, hours = time_factor.shape
+    hops = max(n - 1, 1)
+    return pl.pallas_call(
+        functools.partial(gather_kernel, n, m),
+        out_shape=(
+            jax.ShapeDtypeStruct((n * slots, lags, width), footprints.dtype),
+            jax.ShapeDtypeStruct((n * block, hours), time_factor.dtype),
+            jax.ShapeDtypeStruct((n,) + table.shape, table.dtype),
+        ),
+        in_specs=[pl.BlockSpec(memory_space=pl.ANY)] * 3,
+        out_specs=(pl.BlockSpec(memory_space=pl.ANY),) * 3,
+        scratch_shapes=[pltpu.SemaphoreType.DMA((3,))]
+        + [pltpu.SemaphoreType.DMA((2, hops))] * 6
+        + [pltpu.SemaphoreType.DMA((max(m - 1, 1), 2, hops))] * 2,
+        compiler_params=pltpu.CompilerParams(collective_id=0, has_side_effects=True),
+        name="gathered",
+    )(footprints, time_factor, table)
+
+
+def total_kernel(axes, sizes, term_ref, out_ref, held, came, send_sem, recv_sem):
+    barrier = pltpu.get_barrier_semaphore()
+    for axis, size in zip(axes, sizes):
+        for other in range(1, size):
+            target = lax.rem(lax.axis_index(axis) + other, size)
+            pl.semaphore_signal(barrier, inc=1, device_id={axis: target}, device_id_type=MESH)
+    pl.semaphore_wait(barrier, sum(sizes) - len(sizes))
+    value = term_ref[...]
+    at = 0
+    for stage, (axis, size) in enumerate(zip(axes, sizes)):
+        held[stage] = value
+        copies = []
+        for other in range(1, size):
+            copies.append(
+                pltpu.make_async_remote_copy(
+                    src_ref=held.at[stage],
+                    dst_ref=came.at[at],
+                    send_sem=send_sem.at[at],
+                    recv_sem=recv_sem.at[at],
+                    device_id={axis: lax.rem(lax.axis_index(axis) + other, size)},
+                    device_id_type=MESH,
+                )
+            )
+            at += 1
+        for copy in copies:
+            copy.start()
+        for index, copy in enumerate(copies):
+            copy.wait()
+            value = value + came[at - len(copies) + index]
+    out_ref[...] = value
+
+
+def totals_of(term, axes):
+    sizes = [lax.axis_size(axis) for axis in axes]
+    copies = max(sum(sizes) - len(sizes), 1)
+    length = term.shape[0]
+    wide = -(-length // 128) * 128
+    padded = jnp.broadcast_to(jnp.pad(term, (0, wide - length))[None, :], (8, wide))
+    return pl.pallas_call(
+        functools.partial(total_kernel, axes, sizes),
+        out_shape=jax.ShapeDtypeStruct((8, wide), jnp.float32),
+        in_specs=[pl.BlockSpec(memory_space=pltpu.VMEM)],
+        out_specs=pl.BlockSpec(memory_space=pltpu.VMEM),
+        scratch_shapes=[
+            pltpu.VMEM((len(sizes), 8, wide), jnp.float32),
+            pltpu.VMEM((copies, 8, wide), jnp.float32),
+            pltpu.SemaphoreType.DMA((copies,)),
+            pltpu.SemaphoreType.DMA((copies,)),
+        ],
+        compiler_params=pltpu.CompilerParams(collective_id=1, has_side_effects=True),
+        name="totals",
+    )(padded)[0, :length]
+
+
+def spread_kernel(
+    nt, no, step, factor_ref, grid_ref, out_ref, stage, core_in, chip, far_in, core_send, core_recv, far_send, far_recv
+):
+    tm, core = lax.axis_index("tm"), lax.axis_index("obs")
+    hours, columns = grid_ref.shape
+    own = hours // (nt * no)
+    pieces = columns // step
+    barrier = pltpu.get_barrier_semaphore()
+    for other in range(1, no):
+        pl.semaphore_signal(barrier, inc=1, device_id={"obs": lax.rem(core + other, no)}, device_id_type=MESH)
+    for other in range(1, nt):
+        pl.semaphore_signal(barrier, inc=1, device_id={"tm": lax.rem(tm + other, nt)}, device_id_type=MESH)
+    pl.semaphore_wait(barrier, nt + no - 2)
+
+    def core_copy(piece, other):
+        target = lax.rem(core + other, no)
+        return pltpu.make_async_remote_copy(
+            src_ref=stage.at[piece, target],
+            dst_ref=core_in.at[other - 1, piece],
+            send_sem=core_send.at[other - 1, piece],
+            recv_sem=core_recv.at[other - 1, piece],
+            device_id={"obs": target},
+            device_id_type=MESH,
+        )
+
+    def far_copy(piece, other):
+        target = lax.rem(tm + other, nt)
+        return pltpu.make_async_remote_copy(
+            src_ref=chip.at[piece, target],
+            dst_ref=far_in.at[other - 1, piece],
+            send_sem=far_send.at[other - 1, piece],
+            recv_sem=far_recv.at[other - 1, piece],
+            device_id={"tm": target},
+            device_id_type=MESH,
+        )
+
+    def pair(piece):
+        total = stage[piece, core].astype(jnp.float32)
+        for other in range(1, no):
+            core_copy(piece, other).wait_recv()
+            total = total + core_in[other - 1, piece].astype(jnp.float32)
+        chip[piece] = total.astype(jnp.bfloat16).reshape(nt, own, step)
+        for other in range(1, nt):
+            far_copy(piece, other).start()
+
+    def work(piece, carry):
+        span = pl.ds(pl.multiple_of(piece * step, step), step)
+        product = jnp.dot(factor_ref[...], grid_ref[:, span], preferred_element_type=jnp.float32)
+        product = product.astype(jnp.bfloat16)
+        for j in range(nt):
+            for k in range(no):
+                begin = (j * no + k) * own
+                stage[piece, k, j * own : (j + 1) * own, :] = product[begin : begin + own]
+        for other in range(1, no):
+            core_copy(piece, other).start()
+
+        @pl.when(piece > 0)
+        def _():
+            pair(piece - 1)
+
+        return carry
+
+    lax.fori_loop(0, pieces, work, 0)
+    pair(pieces - 1)
+
+    def last(piece, carry):
+        span = pl.ds(pl.multiple_of(piece * step, step), step)
+        total = chip[piece, tm].astype(jnp.float32)
+        for other in range(1, nt):
+            far_copy(piece, other).wait_recv()
+            total = total + far_in[other - 1, piece].astype(jnp.float32)
+        out_ref[:, span] = total.astype(jnp.bfloat16)
+        for other in range(1, no):
+            core_copy(piece, other).wait_send()
+        for other in range(1, nt):
+            far_copy(piece, other).wait_send()
+        return carry
+
+    lax.fori_loop(0, pieces, last, 0)
+
+
+def spread_of(factor, grid):
+    nt, no = lax.axis_size("tm"), lax.axis_size("obs")
+    hours, columns = grid.shape
+    own = hours // (nt * no)
+    step = chunk_of(columns, 256)
+    pieces = columns // step
+    far, near = max(nt - 1, 1), max(no - 1, 1)
+    return pl.pallas_call(
+        functools.partial(spread_kernel, nt, no, step),
+        out_shape=jax.ShapeDtypeStruct((own, columns), jnp.bfloat16),
+        in_specs=[pl.BlockSpec(memory_space=pltpu.VMEM)] * 2,
+        out_specs=pl.BlockSpec(memory_space=pltpu.VMEM),
+        scratch_shapes=[
+            pltpu.VMEM((pieces, no, nt * own, step), jnp.bfloat16),
+            pltpu.VMEM((near, pieces, nt * own, step), jnp.bfloat16),
+            pltpu.VMEM((pieces, nt, own, step), jnp.bfloat16),
+            pltpu.VMEM((far, pieces, own, step), jnp.bfloat16),
+            pltpu.SemaphoreType.DMA((near, pieces)),
+            pltpu.SemaphoreType.DMA((near, pieces)),
+            pltpu.SemaphoreType.DMA((far, pieces)),
+            pltpu.SemaphoreType.DMA((far, pieces)),
+        ],
+        compiler_params=pltpu.CompilerParams(
+            collective_id=2, has_side_effects=True, vmem_limit_bytes=58 * 1024 * 1024
+        ),
+        name="spread",
+    )(factor, grid)
 
 
 def per_device(
@@ -176,11 +510,10 @@
     observations = obs_weight.shape[0]
     rows = -(-lags // ALIGN) * ALIGN + ALIGN
     own_live = (jnp.arange(slots, dtype=jnp.int32)[:, None] < tile_count).astype(jnp.int32)
-    table = lax.all_gather(
-        jnp.concatenate([tile_obs, tile_block, tile_hour, own_live], axis=1), "space", axis=0, tiled=True
-    )
-    tiles = lax.all_gather(footprints, "space", axis=0, tiled=True)
-    factor = lax.all_gather(time_factor, "space", axis=0, tiled=True)
+    table = jnp.concatenate([tile_obs, tile_block, tile_hour, own_live], axis=1)
+    table = jnp.pad(table, ((0, 0), (0, 128 - table.shape[1])))
+    tiles, factor, table = gathered(footprints, time_factor, table)
+    table = table.reshape(-1, 128)[:, :4]
     full_state = lax.all_gather(state, ("tm", "obs"), axis=0, tiled=True)
     hours = factor.shape[0]
     count = tiles.shape[0]
@@ -204,11 +537,9 @@
     modeled = jnp.where(number < live, jnp.sum(sums, axis=(1, 2)), 0.0)
     onehot = obs[:, None] == jnp.arange(observations, dtype=jnp.int32)[None, :]
     local_totals = jnp.sum(jnp.where(onehot, modeled[:, None], 0.0), axis=0)
-    innovation = obs_weight * lax.psum(local_totals, ("space", "tm", "obs"))
+    innovation = obs_weight * totals_of(local_totals, ("space", "tm", "obs"))
     weight = jnp.sum(jnp.where(onehot, innovation[None, :], 0.0), axis=1)
-    spread = lax.psum_scatter(
-        back_product(base, live, weight, factor, image), ("tm", "obs"), scatter_dimension=0, tiled=True
-    )
+    spread = spread_of(factor, placed(base, live, weight, image, hours))
     return state.astype(jnp.float32) + spread.astype(jnp.float32)
 
 

time: 307 us -> 204 us (0.66)
  waiting for transfers between devices: 173 us -> 0.71 us
  Pallas kernels: 64.1 us -> 174 us
  blocking collectives: 46 us -> 0 us
  local copies, waits for them, and re-layouts: 0.75 us -> 5.3 us
    pallas_call x1 -> x4, Pallas kernels: 19.2 us -> 130 us  [the longest x1 56.2 us: spread_of(): pl.pallas_call(functools.partial(spread_kernel, nt, no, step), out_shape=...]
    reduce_scatter x1 -> x0, waiting for transfers between devices: 69.2 us -> none  [per_device(): lax.psum_scatter(back_product(base, live, weight, factor, image), ('tm',...]
    all_gather x1, waiting for transfers between devices: 58.6 us -> 0.01 us  [per_device(): full_state = lax.all_gather(state, ('tm', 'obs'), axis=0, tiled=True)]
    all_gather x2 -> x0, waiting for transfers between devices: 42.8 us -> none  [the longest x1 22.7 us: per_device(): tiles = lax.all_gather(footprints, 'space', axis=0, tiled=True)]
    psum x1 -> x0, blocking collectives: 32.3 us -> none  [per_device(): innovation = obs_weight * lax.psum(local_totals, ('space', 'tm', 'obs'))]
    all_gather x1 -> x0, blocking collectives: 13.6 us -> none  [per_device(): lax.all_gather(jnp.concatenate([tile_obs, tile_block, tile_hour, own_live...]
  transfers between devices with their start and end apart: 4 -> 1, of which waited for: 4 -> 0; matrix products, arithmetic and copies ran while one was open for 1% -> 3% of each run, Pallas kernels for 9% -> 37%
where the time goes in v2:
time: 204 us; the launch traced here: 203 us
  Pallas kernels  174 us (85%)
  between operations  14.1 us (7%)
  other arithmetic  9.29 us (5%)
  local copies, waits for them, and re-layouts  5.3 us (3%)
    pallas_call x1, Pallas kernels, spread_of(): pl.pallas_call(functools.partial(spread_kernel, nt, no, step), out_shape=...  56.2 us
    pallas_call x1, Pallas kernels, gathered(): pl.pallas_call(functools.partial(gather_kernel, n, m), out_shape=(jax.Sha...  49.8 us
    pallas_call x1, Pallas kernels, images(): pl.pallas_call(functools.partial(image_kernel, lags, rows, step), grid_sp...  25.9 us
    pallas_call x1, Pallas kernels, window_sums(): pl.pallas_call(functools.partial(window_kernel, rows), grid_spec=pltpu.Pr...  18.2 us
    pallas_call x1, Pallas kernels, placed(): pl.pallas_call(functools.partial(place_kernel, rows), grid_spec=pltpu.Pre...  13.8 us
    pallas_call x1, Pallas kernels, totals_of(): pl.pallas_call(functools.partial(total_kernel, axes, sizes), out_shape=ja...  10.1 us
    add x1, other arithmetic, per_device(): return state.astype(jnp.float32) + spread.astype(jnp.float32)  4.33 us
  transfers between devices with their start and end apart: 1, of which 0 were waited for; matrix products, arithmetic and copies ran while one was open for 3% of the time, Pallas kernels for 37%

profile of v2, /device:TPU:0, one launch (start us, length us, event | category | flops | bytes accessed | tf_op | source)
XLA Modules:
  0.0 203.4 jit_solution(16054169918983570224)
XLA Ops:
  6.5 0.0 all-gather.2.cloned.1.call-start
  6.5 0.7 all-gather.2.cloned.1.call-update
  7.9 0.7 copy.17
  8.6 0.7 copy.18
  9.4 0.7 copy.19
  10.1 0.1 pad_add_fusion
  10.2 0.6 pad.8.table_ref
  10.8 49.8 %gathered.1 = (bf16[32,48,512]{2,1,0:T(8,128)(2,1)}, bf16[1024,1024]{1,0:T(8,128)(2,1)}, s32[4,8,128]{2,1,0:T(8,128)}) custom-call(bf16[8,48,512]{2,1,0:T(8,128)(2,1)} %tiles_ref.1, bf16[256,1024]{1,0:T(8,128)(2,1)} %factor_ref.2, s32[8,128]{1,0:T(8,128)} %pad.8.table_ref), custom_call_target="tpu_custom_call" | custom-call | tf_op jit(solution)/shard_map/gathered/pallas_call | solution.py:316
  60.5 0.9 fusion.5
  61.5 0.1 copy.24
  61.6 0.1 copy.25
  61.6 0.1 copy.26
  61.7 0.1 copy.27
  61.8 0.1 convert_reduce_fusion.1.start_ref
  61.9 0.0 copy-start.1
  61.9 0.6 slice.26.live_ref
  62.6 0.2 convert_reduce_fusion
  62.8 0.6 select_reduce_fusion.3
  63.4 0.6 fusion.4
  64.0 0.0 copy-done.1
  64.0 25.9 %images.1.image_ref = bf16[32,64,4096]{2,1,0:T(8,128)(2,1)} custom-call(s32[32]{0:T(128)} %get-tuple-element.12.order_ref, s32[32]{0:T(128)} %get-tuple-element.14.shift_ref, s32[9]{0:T(128)} %copy-done.1, bf16[32,48,512]{2,1,0:T(8,128)(2,1)} %get-tuple-element.10.tiles_ref, bf16[4096,4096]{1,0:T(8,128)(2,1)} %factor_ref.3), custom_call_target="tpu_custom_call" | custom-call | flops 8589934592 | bytes 33554432 | tf_op jit(solution)/shard_map/images/pallas_call | solution.py:60
  89.9 0.0 all-gather.2.cloned.1.call-done.state_ref
  89.9 0.0 copy-start.2
  90.0 18.2 %window_sums.1 = f32[32,8,128]{2,1,0:T(8,128)} custom-call(s32[32]{0:T(128)} %get-tuple-element.15.base_ref, s32[1]{0:T(128)} %slice.26.live_ref, bf16[1024,1024]{1,0:T(8,128)(2,1)} %get-tuple-element.8.factor_ref, bf16[1024,4096]{1,0:T(8,128)(2,1)} %all-gather.2.cloned.1.call-done.state_ref, bf16[32,64,4096]{2,1,0:T(8,128)(2,1)} %images.1.image_ref), custom_call_target="tpu_custom_call" | custom-call | tf_op jit(solution)/shard_map/window_sums/pallas_call | solution.py:106
  108.2 1.2 reduce_sum.77
  109.4 0.6 compare_select_fusion
  110.1 0.1 select_reduce_fusion.1
  110.2 0.6 broadcast_in_dim.32.term_ref
  110.7 10.1 %totals.1 = f32[8,128]{1,0:T(8,128)} custom-call(f32[8,128]{1,0:T(8,128)} %broadcast_in_dim.32.term_ref), custom_call_target="tpu_custom_call" | custom-call | tf_op jit(solution)/shard_map/totals/pallas_call | solution.py:371
  120.8 0.0 copy-done.2
  120.8 0.7 bitcast_multiply_fusion
  121.5 0.7 select_reduce_fusion.weight_ref
  122.2 13.8 %placed.1.grid_ref = bf16[1024,4096]{1,0:T(8,128)(2,1)} custom-call(s32[32]{0:T(128)} %get-tuple-element.15.base_ref, s32[1]{0:T(128)} %slice.26.live_ref, f32[32]{0:T(128)} %select_reduce_fusion.weight_ref, bf16[32,64,4096]{2,1,0:T(8,128)(2,1)} %images.1.image_ref), custom_call_target="tpu_custom_call" | custom-call | tf_op jit(solution)/shard_map/placed/pallas_call | solution.py:140
  136.0 0.0 copy-start
  136.0 56.2 %spread.1 = bf16[256,4096]{1,0:T(8,128)(2,1)} custom-call(bf16[1024,1024]{1,0:T(8,128)(2,1)} %get-tuple-element.8.factor_ref, bf16[1024,4096]{1,0:T(8,128)(2,1)} %placed.1.grid_ref), custom_call_target="tpu_custom_call" | custom-call | tf_op jit(solution)/shard_map/spread/pallas_call | solution.py:475
  192.2 0.0 copy-done
  192.2 4.3 %convert_add_fusion = f32[256,4096]{1,0:T(8,128)} fusion(bf16[256,4096]{1,0:T(8,128)(2,1)} %spread.1, bf16[256,4096]{1,0:T(8,128)(2,1)S(1)} %copy-done), kind=kLoop, calls=%fused_computation | loop fusion | flops 3145728 | bytes 8388608 | tf_op jit(solution)/shard_map/add | solution.py:543
  (3 shorter events, 0.0 us)
Async XLA Ops:
  6.5 83.4 %all-gather.2.cloned.1.call-start = ((), (), s32[]{:S(2)}) async-start(), calls=%async_computation | async-start | bytes 10485760 | tf_op jit(solution)/shard_map/all_gather | solution.py:517
  61.9 2.1 %copy-start.1 = (s32[9]{0:T(128)}, s32[9]{0:T(128)S(1)}, u32[]{:S(2)}) copy-start(s32[9]{0:T(128)S(1)} %convert_reduce_fusion.1.start_ref) | copy-start | bytes 112
  89.9 30.9 %copy-start.2 = (f32[32]{0:T(128)S(1)}, f32[32]{0:T(128)}, u32[]{:S(2)}) copy-start(f32[32]{0:T(128)} %param.17) | copy-start | bytes 388
  136.0 56.2 %copy-start = (bf16[256,4096]{1,0:T(8,128)(2,1)S(1)}, bf16[256,4096]{1,0:T(8,128)(2,1)}, u32[]{:S(2)}) copy-start(bf16[256,4096]{1,0:T(8,128)(2,1)} %param.9) | copy-start | bytes 6291460
Sparse Core Ops, SparseCore 0:
  8.9 60.9 all-gather.1

commit v3 on v2

--- a/solution.py
+++ b/solution.py
@@ -19,15 +19,37 @@
     return chunk
 
 
-def image_kernel(lags, rows, step, order_ref, shift_ref, start_ref, tiles_ref, factor_ref, image_ref, held):
+def image_kernel(
+    lags, rows, step, order_ref, shift_ref, start_ref, tiles_ref, factor_ref, image_ref, held, made, busy, made_sem
+):
     block = pl.program_id(0)
     begin, end = start_ref[block], start_ref[block + 1]
     last = order_ref.shape[0] - 1
     width = tiles_ref.shape[2]
     columns = factor_ref.shape[1]
 
+    def out_copy(slot, k, at):
+        return pltpu.make_async_copy(made.at[slot, k], image_ref.at[at], made_sem.at[slot, k])
+
+    def settle(slot):
+        for k in range(GROUP):
+
+            @pl.when(busy[slot * GROUP + k] == 1)
+            def _():
+                out_copy(slot, k, 0).wait()
+                busy[slot * GROUP + k] = 0
+
+    @pl.when(block == 0)
+    def _():
+        for k in range(2 * GROUP):
+            busy[k] = 0
+        busy[2 * GROUP] = 0
+
     def group(index, carry):
         first = begin + index * GROUP
+        slot = busy[2 * GROUP]
+        busy[2 * GROUP] = 1 - slot
+        settle(slot)
         for k in range(GROUP):
             at = jnp.minimum(first + k, last)
             tile = tiles_ref[order_ref[at]].astype(jnp.float32)
@@ -38,19 +60,25 @@
         def part(piece, inner):
             span = pl.ds(pl.multiple_of(piece * step, step), step)
             product = jnp.dot(held[...], factor_ref[:, span], preferred_element_type=jnp.float32)
-            product = product.astype(jnp.bfloat16)
-            for k in range(GROUP):
-
-                @pl.when(first + k < end)
-                def _():
-                    image_ref[first + k, :, span] = product[k * rows : (k + 1) * rows]
-
+            made[slot, :, :, span] = product.astype(jnp.bfloat16).reshape(GROUP, rows, step)
             return inner
 
         lax.fori_loop(0, columns // step, part, 0)
+        for k in range(GROUP):
+
+            @pl.when(first + k < end)
+            def _():
+                out_copy(slot, k, first + k).start()
+                busy[slot * GROUP + k] = 1
+
         return carry
 
     lax.fori_loop(0, (end - begin + GROUP - 1) // GROUP, group, 0)
+
+    @pl.when(block == pl.num_programs(0) - 1)
+    def _():
+        settle(0)
+        settle(1)
 
 
 def images(order, shift, start, tiles, factor, rows):
@@ -66,8 +94,13 @@
                 pl.BlockSpec((count, lags, width), lambda i, *_: (0, 0, 0)),
                 pl.BlockSpec((width, columns), lambda i, *_: (i, 0)),
             ],
-            out_specs=pl.BlockSpec((count, rows, columns), lambda i, *_: (0, 0, 0)),
-            scratch_shapes=[pltpu.VMEM((GROUP * rows, width), jnp.bfloat16)],
+            out_specs=pl.BlockSpec(memory_space=pl.ANY),
+            scratch_shapes=[
+                pltpu.VMEM((GROUP * rows, width), jnp.bfloat16),
+                pltpu.VMEM((2, GROUP, rows, columns), jnp.bfloat16),
+                pltpu.SMEM((2 * GROUP + 1,), jnp.int32),
+                pltpu.SemaphoreType.DMA((2, GROUP)),
+            ],
         ),
         out_shape=jax.ShapeDtypeStruct((count, rows, columns), jnp.bfloat16),
         compiler_params=pltpu.CompilerParams(vmem_limit_bytes=58 * 1024 * 1024),
@@ -155,6 +188,7 @@
 def gather_kernel(
     n,
     m,
+    g,
     tiles_ref,
     factor_ref,
     table_ref,
@@ -171,9 +205,11 @@
     core_send,
     core_recv,
 ):
-    me, core = lax.axis_index("space"), lax.axis_index("obs")
+    me, obs, side = lax.axis_index("space"), lax.axis_index("obs"), lax.axis_index("groups")
+    core = side * m + obs
     slots, block = tiles_ref.shape[0], factor_ref.shape[0]
-    part = block // m
+    part = block // (m * g)
+    others = [(i, j) for i in range(g) for j in range(m) if i or j]
     barrier = pltpu.get_barrier_semaphore()
     ways = (1, -1)
 
@@ -186,10 +222,15 @@
         def _():
             pl.semaphore_signal(barrier, inc=1, device_id={"space": me + way}, device_id_type=MESH)
 
-    for other in range(1, m):
-        pl.semaphore_signal(barrier, inc=1, device_id={"obs": lax.rem(core + other, m)}, device_id_type=MESH)
+    for i, j in others:
+        pl.semaphore_signal(
+            barrier,
+            inc=1,
+            device_id={"groups": lax.rem(side + i, g), "obs": lax.rem(obs + j, m)},
+            device_id_type=MESH,
+        )
     ends = jnp.where(me > 0, 1, 0) + jnp.where(me < n - 1, 1, 0)
-    pl.semaphore_wait(barrier, ends + (m - 1))
+    pl.semaphore_wait(barrier, ends + len(others))
 
     def tile_rows(index):
         return tiles_out.at[pl.ds(index * slots, slots)]
@@ -242,9 +283,9 @@
         return pltpu.make_async_remote_copy(
             src_ref=part_rows(index, which),
             dst_ref=part_rows(index, which),
-            send_sem=core_send.at[other - 1, d, k],
-            recv_sem=core_recv.at[other - 1, d, k],
-            device_id={"obs": lax.rem(core + other, m)},
+            send_sem=core_send.at[other, d, k],
+            recv_sem=core_recv.at[other, d, k],
+            device_id={"groups": lax.rem(side + others[other][0], g), "obs": lax.rem(obs + others[other][1], m)},
             device_id_type=MESH,
         )
 
@@ -281,7 +322,7 @@
 
                 @pl.when(inside(me - way * k))
                 def _():
-                    for other in range(1, m):
+                    for other in range(len(others)):
                         core_copy(d, k - 1, other, me - way * k, core).start()
 
     for k in range(1, n):
@@ -289,8 +330,9 @@
 
             @pl.when(inside(me - way * k))
             def _():
-                for other in range(1, m):
-                    came = core_copy(d, k - 1, other, me - way * k, lax.rem(core + m - other, m))
+                for other, (i, j) in enumerate(others):
+                    source = lax.rem(side + g - i, g) * m + lax.rem(obs + m - j, m)
+                    came = core_copy(d, k - 1, other, me - way * k, source)
                     came.wait_recv()
                     core_copy(d, k - 1, other, me - way * k, core).wait_send()
 
@@ -309,12 +351,12 @@
 
 
 def gathered(footprints, time_factor, table):
-    n, m = lax.axis_size("space"), lax.axis_size("obs")
+    n, m, g = lax.axis_size("space"), lax.axis_size("obs"), lax.axis_size("groups")
     slots, lags, width = footprints.shape
     block, hours = time_factor.shape
     hops = max(n - 1, 1)
     return pl.pallas_call(
-        functools.partial(gather_kernel, n, m),
+        functools.partial(gather_kernel, n, m, g),
         out_shape=(
             jax.ShapeDtypeStruct((n * slots, lags, width), footprints.dtype),
             jax.ShapeDtypeStruct((n * block, hours), time_factor.dtype),
@@ -324,20 +366,24 @@
         out_specs=(pl.BlockSpec(memory_space=pl.ANY),) * 3,
         scratch_shapes=[pltpu.SemaphoreType.DMA((3,))]
         + [pltpu.SemaphoreType.DMA((2, hops))] * 6
-        + [pltpu.SemaphoreType.DMA((max(m - 1, 1), 2, hops))] * 2,
+        + [pltpu.SemaphoreType.DMA((max(m * g - 1, 1), 2, hops))] * 2,
         compiler_params=pltpu.CompilerParams(collective_id=0, has_side_effects=True),
         name="gathered",
     )(footprints, time_factor, table)
 
 
-def total_kernel(axes, sizes, term_ref, out_ref, held, came, send_sem, recv_sem):
+def total_kernel(axes, sizes, sums_ref, obs_ref, gain_ref, out_ref, held, came, send_sem, recv_sem):
     barrier = pltpu.get_barrier_semaphore()
     for axis, size in zip(axes, sizes):
         for other in range(1, size):
             target = lax.rem(lax.axis_index(axis) + other, size)
             pl.semaphore_signal(barrier, inc=1, device_id={axis: target}, device_id_type=MESH)
     pl.semaphore_wait(barrier, sum(sizes) - len(sizes))
-    value = term_ref[...]
+    count, wide = out_ref.shape[0], gain_ref.shape[1]
+    modeled = jnp.sum(jnp.sum(sums_ref[...], axis=1), axis=1, keepdims=True)
+    onehot = obs_ref[:, :1] == lax.broadcasted_iota(jnp.int32, (count, wide), 1)
+    value = jnp.sum(jnp.where(onehot, modeled, 0.0), axis=0, keepdims=True)
+    value = jnp.broadcast_to(value, (8, wide))
     at = 0
     for stage, (axis, size) in enumerate(zip(axes, sizes)):
         held[stage] = value
@@ -359,19 +405,22 @@
         for index, copy in enumerate(copies):
             copy.wait()
             value = value + came[at - len(copies) + index]
-    out_ref[...] = value
-
-
-def totals_of(term, axes):
+    innovation = gain_ref[:1] * value[:1]
+    weight = jnp.sum(jnp.where(onehot, innovation, 0.0), axis=1, keepdims=True)
+    out_ref[...] = jnp.broadcast_to(weight, out_ref.shape)
+
+
+def weights_of(sums, obs, gain, axes):
     sizes = [lax.axis_size(axis) for axis in axes]
     copies = max(sum(sizes) - len(sizes), 1)
-    length = term.shape[0]
+    length, count = gain.shape[0], obs.shape[0]
     wide = -(-length // 128) * 128
-    padded = jnp.broadcast_to(jnp.pad(term, (0, wide - length))[None, :], (8, wide))
+    gain = jnp.broadcast_to(jnp.pad(gain, (0, wide - length))[None, :], (8, wide))
+    obs = jnp.broadcast_to(obs[:, None], (count, 128))
     return pl.pallas_call(
         functools.partial(total_kernel, axes, sizes),
-        out_shape=jax.ShapeDtypeStruct((8, wide), jnp.float32),
-        in_specs=[pl.BlockSpec(memory_space=pltpu.VMEM)],
+        out_shape=jax.ShapeDtypeStruct((count, 128), jnp.float32),
+        in_specs=[pl.BlockSpec(memory_space=pltpu.VMEM)] * 3,
         out_specs=pl.BlockSpec(memory_space=pltpu.VMEM),
         scratch_shapes=[
             pltpu.VMEM((len(sizes), 8, wide), jnp.float32),
@@ -381,16 +430,41 @@
         ],
         compiler_params=pltpu.CompilerParams(collective_id=1, has_side_effects=True),
         name="totals",
-    )(padded)[0, :length]
+    )(sums, obs, gain)[:, 0]
 
 
 def spread_kernel(
-    nt, no, step, factor_ref, grid_ref, out_ref, stage, core_in, chip, far_in, core_send, core_recv, far_send, far_recv
+    nt,
+    no,
+    step,
+    factor_ref,
+    grid_ref,
+    out_ref,
+    stage,
+    core_in,
+    chip,
+    far_in,
+    near_grid,
+    grid_sem,
+    core_send,
+    core_recv,
+    far_send,
+    far_recv,
 ):
     tm, core = lax.axis_index("tm"), lax.axis_index("obs")
     hours, columns = grid_ref.shape
     own = hours // (nt * no)
     pieces = columns // step
+
+    def fetch(piece):
+        span = pl.ds(pl.multiple_of(piece * step, step), step)
+        return pltpu.make_async_copy(grid_ref.at[:, span], near_grid.at[piece], grid_sem.at[piece])
+
+    def begin(piece, carry):
+        fetch(piece).start()
+        return carry
+
+    lax.fori_loop(0, pieces, begin, 0)
     barrier = pltpu.get_barrier_semaphore()
     for other in range(1, no):
         pl.semaphore_signal(barrier, inc=1, device_id={"obs": lax.rem(core + other, no)}, device_id_type=MESH)
@@ -430,13 +504,13 @@
             far_copy(piece, other).start()
 
     def work(piece, carry):
-        span = pl.ds(pl.multiple_of(piece * step, step), step)
-        product = jnp.dot(factor_ref[...], grid_ref[:, span], preferred_element_type=jnp.float32)
+        fetch(piece).wait()
+        product = jnp.dot(factor_ref[...], near_grid[piece], preferred_element_type=jnp.float32)
         product = product.astype(jnp.bfloat16)
         for j in range(nt):
             for k in range(no):
-                begin = (j * no + k) * own
-                stage[piece, k, j * own : (j + 1) * own, :] = product[begin : begin + own]
+                row = (j * no + k) * own
+                stage[piece, k, j * own : (j + 1) * own, :] = product[row : row + own]
         for other in range(1, no):
             core_copy(piece, other).start()
 
@@ -475,13 +549,15 @@
     return pl.pallas_call(
         functools.partial(spread_kernel, nt, no, step),
         out_shape=jax.ShapeDtypeStruct((own, columns), jnp.bfloat16),
-        in_specs=[pl.BlockSpec(memory_space=pltpu.VMEM)] * 2,
+        in_specs=[pl.BlockSpec(memory_space=pltpu.VMEM), pl.BlockSpec(memory_space=pl.ANY)],
         out_specs=pl.BlockSpec(memory_space=pltpu.VMEM),
         scratch_shapes=[
             pltpu.VMEM((pieces, no, nt * own, step), jnp.bfloat16),
             pltpu.VMEM((near, pieces, nt * own, step), jnp.bfloat16),
             pltpu.VMEM((pieces, nt, own, step), jnp.bfloat16),
             pltpu.VMEM((far, pieces, own, step), jnp.bfloat16),
+            pltpu.VMEM((pieces, hours, step), jnp.bfloat16),
+            pltpu.SemaphoreType.DMA((pieces,)),
             pltpu.SemaphoreType.DMA((near, pieces)),
             pltpu.SemaphoreType.DMA((near, pieces)),
             pltpu.SemaphoreType.DMA((far, pieces)),
@@ -507,7 +583,6 @@
 ):
     slots, lags, width = footprints.shape
     blocks = spatial_factor.shape[0] // width
-    observations = obs_weight.shape[0]
     rows = -(-lags // ALIGN) * ALIGN + ALIGN
     own_live = (jnp.arange(slots, dtype=jnp.int32)[:, None] < tile_count).astype(jnp.int32)
     table = jnp.concatenate([tile_obs, tile_block, tile_hour, own_live], axis=1)
@@ -534,11 +609,7 @@
 
     image = images(order, shift, start, tiles, spatial_factor, rows)
     sums = window_sums(base, live, factor, full_state, image)
-    modeled = jnp.where(number < live, jnp.sum(sums, axis=(1, 2)), 0.0)
-    onehot = obs[:, None] == jnp.arange(observations, dtype=jnp.int32)[None, :]
-    local_totals = jnp.sum(jnp.where(onehot, modeled[:, None], 0.0), axis=0)
-    innovation = obs_weight * totals_of(local_totals, ("space", "tm", "obs"))
-    weight = jnp.sum(jnp.where(onehot, innovation[None, :], 0.0), axis=1)
+    weight = weights_of(sums, obs, obs_weight, ("space", "tm", "obs"))
     spread = spread_of(factor, placed(base, live, weight, image, hours))
     return state.astype(jnp.float32) + spread.astype(jnp.float32)
 

time: 204 us -> 196 us (0.961)
  Pallas kernels: 174 us -> 168 us
  other arithmetic: 9.29 us -> 5.97 us
  local copies, waits for them, and re-layouts: 5.3 us -> 7.95 us
    pallas_call x1, Pallas kernels: 25.9 us -> 22 us  [images(): pl.pallas_call(functools.partial(image_kernel, lags, rows, step), grid_sp...]
    pallas_call x1, Pallas kernels: 56.2 us -> 53.9 us  [spread_of(): pl.pallas_call(functools.partial(spread_kernel, nt, no, step), out_shape=...]
  transfers between devices with their start and end apart: 1 -> 1, of which waited for: 0 -> 0; matrix products, arithmetic and copies ran while one was open for 3% -> 4% of each run, Pallas kernels for 37% -> 34%
where the time goes in v3:
time: 196 us
  Pallas kernels  168 us (86%)
  between operations  14.1 us (7%)
  local copies, waits for them, and re-layouts  7.95 us (4%)
  other arithmetic  5.97 us (3%)
    pallas_call x1, Pallas kernels, spread_of(): pl.pallas_call(functools.partial(spread_kernel, nt, no, step), out_shape=...  53.9 us
    pallas_call x1, Pallas kernels, gathered(): pl.pallas_call(functools.partial(gather_kernel, n, m, g), out_shape=(jax....  45.5 us
    pallas_call x1, Pallas kernels, images(): pl.pallas_call(functools.partial(image_kernel, lags, rows, step), grid_sp...  22 us
    pallas_call x1, Pallas kernels, window_sums(): pl.pallas_call(functools.partial(window_kernel, rows), grid_spec=pltpu.Pr...  18.1 us
    pallas_call x1, Pallas kernels, weights_of(): pl.pallas_call(functools.partial(total_kernel, axes, sizes), out_shape=ja...  14.3 us
    pallas_call x1, Pallas kernels, placed(): pl.pallas_call(functools.partial(place_kernel, rows), grid_spec=pltpu.Pre...  13.7 us
    add x1, other arithmetic, per_device(): return state.astype(jnp.float32) + spread.astype(jnp.float32)  4.33 us
  transfers between devices with their start and end apart: 1, of which 0 were waited for; matrix products, arithmetic and copies ran while one was open for 4% of the time, Pallas kernels for 34%

profile of v3, /device:TPU:0, one launch (start us, length us, event | category | flops | bytes accessed | tf_op | source)
XLA Modules:
  0.0 196.3 jit_solution(5997388850438242806)
XLA Ops:
  6.5 0.0 all-gather.2.cloned.1.call-start
  6.5 0.7 all-gather.2.cloned.1.call-update
  7.9 0.7 copy.24
  8.6 0.7 copy.25
  9.4 0.7 copy.26
  10.1 0.1 pad_add_fusion
  10.2 0.6 pad.8.table_ref
  10.8 45.5 %gathered.1 = (bf16[32,48,512]{2,1,0:T(8,128)(2,1)}, bf16[1024,1024]{1,0:T(8,128)(2,1)}, s32[4,8,128]{2,1,0:T(8,128)}) custom-call(bf16[8,48,512]{2,1,0:T(8,128)(2,1)} %tiles_ref.1, bf16[256,1024]{1,0:T(8,128)(2,1)} %factor_ref.2, s32[8,128]{1,0:T(8,128)} %pad.8.table_ref), custom_call_target="tpu_custom_call" | custom-call | tf_op jit(solution)/shard_map/gathered/pallas_call | solution.py:358
  56.3 0.9 fusion.5
  57.2 0.1 copy.31
  57.3 0.1 copy.32
  57.4 0.1 copy.33
  57.5 0.1 copy.34
  57.5 0.1 convert_reduce_fusion.1.start_ref
  57.7 0.0 copy-start.1
  57.7 0.6 slice.26.live_ref
  58.3 0.7 pad.9
  59.0 0.2 convert_reduce_fusion
  59.2 0.6 select_reduce_fusion
  59.8 0.6 fusion.4
  60.4 0.0 copy-done.1
  60.4 22.0 %images.1.image_ref = bf16[32,64,4096]{2,1,0:T(8,128)(2,1)} custom-call(s32[32]{0:T(128)} %get-tuple-element.12.order_ref, s32[32]{0:T(128)} %get-tuple-element.14.shift_ref, s32[9]{0:T(128)} %copy-done.1, bf16[32,48,512]{2,1,0:T(8,128)(2,1)} %get-tuple-element.10.tiles_ref, bf16[4096,4096]{1,0:T(8,128)(2,1)} %factor_ref.3), custom_call_target="tpu_custom_call" | custom-call | flops 8589934592 | bytes 33554432 | tf_op jit(solution)/shard_map/images/pallas_call | solution.py:88
  82.4 0.0 all-gather.2.cloned.1.call-done.state_ref
  82.4 18.1 %window_sums.1.sums_ref = f32[32,8,128]{2,1,0:T(8,128)} custom-call(s32[32]{0:T(128)} %get-tuple-element.15.base_ref, s32[1]{0:T(128)} %slice.26.live_ref, bf16[1024,1024]{1,0:T(8,128)(2,1)} %get-tuple-element.8.factor_ref, bf16[1024,4096]{1,0:T(8,128)(2,1)} %all-gather.2.cloned.1.call-done.state_ref, bf16[32,64,4096]{2,1,0:T(8,128)(2,1)} %images.1.image_ref), custom_call_target="tpu_custom_call" | custom-call | tf_op jit(solution)/shard_map/window_sums/pallas_call | solution.py:139
  100.6 0.7 broadcast_in_dim.9.obs_ref
  101.2 0.6 broadcast_in_dim.10.gain_ref
  101.8 14.3 %totals.1 = f32[32,128]{1,0:T(8,128)} custom-call(f32[32,8,128]{2,1,0:T(8,128)} %window_sums.1.sums_ref, s32[32,128]{1,0:T(8,128)} %broadcast_in_dim.9.obs_ref, f32[8,128]{1,0:T(8,128)} %broadcast_in_dim.10.gain_ref), custom_call_target="tpu_custom_call" | custom-call | tf_op jit(solution)/shard_map/totals/pallas_call | solution.py:420
  116.1 1.3 slice_reduce_fusion.weight_ref
  117.5 13.7 %placed.1.grid_ref = bf16[1024,4096]{1,0:T(8,128)(2,1)} custom-call(s32[32]{0:T(128)} %get-tuple-element.15.base_ref, s32[1]{0:T(128)} %slice.26.live_ref, f32[32]{0:T(128)} %slice_reduce_fusion.weight_ref, bf16[32,64,4096]{2,1,0:T(8,128)(2,1)} %images.1.image_ref), custom_call_target="tpu_custom_call" | custom-call | tf_op jit(solution)/shard_map/placed/pallas_call | solution.py:173
  131.2 0.0 copy-start
  131.2 53.9 %spread.1 = bf16[256,4096]{1,0:T(8,128)(2,1)} custom-call(bf16[1024,1024]{1,0:T(8,128)(2,1)} %get-tuple-element.8.factor_ref, bf16[1024,4096]{1,0:T(8,128)(2,1)} %placed.1.grid_ref), custom_call_target="tpu_custom_call" | custom-call | tf_op jit(solution)/shard_map/spread/pallas_call | solution.py:549
  185.1 0.0 copy-done
  185.2 4.3 %convert_add_fusion = f32[256,4096]{1,0:T(8,128)} fusion(bf16[256,4096]{1,0:T(8,128)(2,1)} %spread.1, bf16[256,4096]{1,0:T(8,128)(2,1)S(1)} %copy-done), kind=kLoop, calls=%fused_computation | loop fusion | flops 3145728 | bytes 8388608 | tf_op jit(solution)/shard_map/add | solution.py:614
  (2 shorter events, 0.0 us)
Async XLA Ops:
  6.5 75.9 %all-gather.2.cloned.1.call-start = ((), (), s32[]{:S(2)}) async-start(), calls=%async_computation | async-start | bytes 10485760 | tf_op jit(solution)/shard_map/all_gather | solution.py:592
  57.7 2.7 %copy-start.1 = (s32[9]{0:T(128)}, s32[9]{0:T(128)S(1)}, u32[]{:S(2)}) copy-start(s32[9]{0:T(128)S(1)} %convert_reduce_fusion.1.start_ref) | copy-start | bytes 112
  131.2 54.0 %copy-start = (bf16[256,4096]{1,0:T(8,128)(2,1)S(1)}, bf16[256,4096]{1,0:T(8,128)(2,1)}, u32[]{:S(2)}) copy-start(bf16[256,4096]{1,0:T(8,128)(2,1)} %param.9) | copy-start | bytes 6291460
Sparse Core Ops, SparseCore 0:
  8.9 60.9 all-gather.1

commit v4 on v3

--- a/solution.py
+++ b/solution.py
@@ -135,7 +135,7 @@
 def window_sums(base, live, factor, state, image):
     hours, columns = state.shape
     count, rows, _ = image.shape
-    step = chunk_of(columns, 512)
+    step = chunk_of(columns, 1024)
     return pl.pallas_call(
         functools.partial(window_kernel, rows),
         grid_spec=pltpu.PrefetchScalarGridSpec(
@@ -169,7 +169,7 @@
 
 def placed(base, live, weight, image, hours):
     count, rows, columns = image.shape
-    step = chunk_of(columns, 512)
+    step = chunk_of(columns, 1024)
     return pl.pallas_call(
         functools.partial(place_kernel, rows),
         grid_spec=pltpu.PrefetchScalarGridSpec(
@@ -584,23 +584,23 @@
     slots, lags, width = footprints.shape
     blocks = spatial_factor.shape[0] // width
     rows = -(-lags // ALIGN) * ALIGN + ALIGN
-    own_live = (jnp.arange(slots, dtype=jnp.int32)[:, None] < tile_count).astype(jnp.int32)
-    table = jnp.concatenate([tile_obs, tile_block, tile_hour, own_live], axis=1)
-    table = jnp.pad(table, ((0, 0), (0, 128 - table.shape[1])))
+    own_live = (jnp.arange(slots, dtype=jnp.int32) < tile_count[0, 0]).astype(jnp.int32)
+    table = jnp.stack([tile_obs[:, 0], tile_block[:, 0], tile_hour[:, 0], own_live])
+    table = jnp.pad(table, ((0, 4), (0, 128 - slots)))
     tiles, factor, table = gathered(footprints, time_factor, table)
-    table = table.reshape(-1, 128)[:, :4]
+    tile_obs, tile_block, tile_hour, tile_live = [table[:, row, :slots].reshape(-1) for row in range(4)]
     full_state = lax.all_gather(state, ("tm", "obs"), axis=0, tiled=True)
     hours = factor.shape[0]
     count = tiles.shape[0]
 
-    key = jnp.where(table[:, 3] > 0, table[:, 1], blocks)
+    key = jnp.where(tile_live > 0, tile_block, blocks)
     number = jnp.arange(count, dtype=jnp.int32)
     before = (key[None, :] < key[:, None]) | ((key[None, :] == key[:, None]) & (number[None, :] < number[:, None]))
     rank = jnp.sum(before.astype(jnp.int32), axis=1)
     at_rank = (rank[None, :] == number[:, None]).astype(jnp.int32)
     order = jnp.sum(at_rank * number[None, :], axis=1)
-    hour = jnp.sum(at_rank * table[:, 2][None, :], axis=1)
-    obs = jnp.sum(at_rank * table[:, 0][None, :], axis=1)
+    hour = jnp.sum(at_rank * tile_hour[None, :], axis=1)
+    obs = jnp.sum(at_rank * tile_obs[None, :], axis=1)
     edges = jnp.arange(blocks + 1, dtype=jnp.int32)
     start = jnp.sum((key[None, :] < edges[:, None]).astype(jnp.int32), axis=1)
     live = start[blocks:]

time: 196 us -> 192 us (0.980)
  Pallas kernels: 168 us -> 164 us
  local copies, waits for them, and re-layouts: 7.95 us -> 4.76 us
    pallas_call x1, Pallas kernels: 14.3 us -> 11.3 us  [weights_of(): pl.pallas_call(functools.partial(total_kernel, axes, sizes), out_shape=ja...]
    unnamed x11 -> x4, local copies, waits for them, and re-layouts: 2.5 us -> 0.01 us
    pallas_call x1, Pallas kernels: 13.7 us -> 11.7 us  [placed(): pl.pallas_call(functools.partial(place_kernel, rows), grid_spec=pltpu.Pre...]
  transfers between devices with their start and end apart: 1 -> 1, of which waited for: 0 -> 0; matrix products, arithmetic and copies ran while one was open for 4% -> 3% of each run, Pallas kernels for 34% -> 36%
where the time goes in v4:
time: 192 us; the launch traced here: 191 us
  Pallas kernels  164 us (85%)
  between operations  14.1 us (7%)
  other arithmetic  7.47 us (4%)
  local copies, waits for them, and re-layouts  4.76 us (2%)
    pallas_call x1, Pallas kernels, spread_of(): pl.pallas_call(functools.partial(spread_kernel, nt, no, step), out_shape=...  54.6 us
    pallas_call x1, Pallas kernels, gathered(): pl.pallas_call(functools.partial(gather_kernel, n, m, g), out_shape=(jax....  45.5 us
    pallas_call x1, Pallas kernels, images(): pl.pallas_call(functools.partial(image_kernel, lags, rows, step), grid_sp...  23.8 us
    pallas_call x1, Pallas kernels, window_sums(): pl.pallas_call(functools.partial(window_kernel, rows), grid_spec=pltpu.Pr...  17.2 us
    pallas_call x1, Pallas kernels, placed(): pl.pallas_call(functools.partial(place_kernel, rows), grid_spec=pltpu.Pre...  11.7 us
    pallas_call x1, Pallas kernels, weights_of(): pl.pallas_call(functools.partial(total_kernel, axes, sizes), out_shape=ja...  11.3 us
    add x1, other arithmetic, per_device(): return state.astype(jnp.float32) + spread.astype(jnp.float32)  4.33 us
  transfers between devices with their start and end apart: 1, of which 0 were waited for; matrix products, arithmetic and copies ran while one was open for 3% of the time, Pallas kernels for 36%

profile of v4, /device:TPU:0, one launch (start us, length us, event | category | flops | bytes accessed | tf_op | source)
XLA Modules:
  0.0 191.3 jit_solution(3712608510920783593)
XLA Ops:
  6.5 0.0 all-gather.2.cloned.1.call-start
  6.5 0.7 all-gather.2.cloned.1.call-update
  7.9 0.7 pad_add_fusion
  8.6 0.6 pad.8.table_ref
  9.2 45.5 %gathered.1 = (bf16[32,48,512]{2,1,0:T(8,128)(2,1)}, bf16[1024,1024]{1,0:T(8,128)(2,1)}, s32[4,8,128]{2,1,0:T(8,128)}) custom-call(bf16[8,48,512]{2,1,0:T(8,128)(2,1)} %tiles_ref.1, bf16[256,1024]{1,0:T(8,128)(2,1)} %factor_ref.2, s32[8,128]{1,0:T(8,128)} %pad.8.table_ref), custom_call_target="tpu_custom_call" | custom-call | tf_op jit(solution)/shard_map/gathered/pallas_call | solution.py:358
  54.7 0.9 slice_reduce_fusion.1
  55.6 0.1 select_n.21
  55.7 0.1 mul.30
  55.8 0.1 mul.35
  55.9 0.1 convert_reduce_fusion.1.start_ref
  56.0 0.0 copy-start.1
  56.0 0.6 slice.21.live_ref
  56.6 0.7 pad.9
  57.3 0.2 convert_reduce_fusion
  57.5 0.6 select_reduce_fusion
  58.1 0.6 fusion.3
  58.7 0.0 copy-done.1
  58.7 23.8 %images.1.image_ref = bf16[32,64,4096]{2,1,0:T(8,128)(2,1)} custom-call(s32[32]{0:T(128)} %get-tuple-element.15.order_ref, s32[32]{0:T(128)} %get-tuple-element.17.shift_ref, s32[9]{0:T(128)} %copy-done.1, bf16[32,48,512]{2,1,0:T(8,128)(2,1)} %get-tuple-element.10.tiles_ref, bf16[4096,4096]{1,0:T(8,128)(2,1)} %factor_ref.3), custom_call_target="tpu_custom_call" | custom-call | flops 8589934592 | bytes 33554432 | tf_op jit(solution)/shard_map/images/pallas_call | solution.py:88
  82.5 0.0 all-gather.2.cloned.1.call-done.state_ref
  82.6 17.2 %window_sums.1.sums_ref = f32[32,8,128]{2,1,0:T(8,128)} custom-call(s32[32]{0:T(128)} %get-tuple-element.18.base_ref, s32[1]{0:T(128)} %slice.21.live_ref, bf16[1024,1024]{1,0:T(8,128)(2,1)} %get-tuple-element.8.factor_ref, bf16[1024,4096]{1,0:T(8,128)(2,1)} %all-gather.2.cloned.1.call-done.state_ref, bf16[32,64,4096]{2,1,0:T(8,128)(2,1)} %images.1.image_ref), custom_call_target="tpu_custom_call" | custom-call | tf_op jit(solution)/shard_map/window_sums/pallas_call | solution.py:139
  99.8 0.7 broadcast_in_dim.9.obs_ref
  100.5 0.6 broadcast_in_dim.10.gain_ref
  101.1 11.3 %totals.1 = f32[32,128]{1,0:T(8,128)} custom-call(f32[32,8,128]{2,1,0:T(8,128)} %window_sums.1.sums_ref, s32[32,128]{1,0:T(8,128)} %broadcast_in_dim.9.obs_ref, f32[8,128]{1,0:T(8,128)} %broadcast_in_dim.10.gain_ref), custom_call_target="tpu_custom_call" | custom-call | tf_op jit(solution)/shard_map/totals/pallas_call | solution.py:420
  112.4 1.3 slice_reduce_fusion.weight_ref
  113.8 11.7 %placed.1.grid_ref = bf16[1024,4096]{1,0:T(8,128)(2,1)} custom-call(s32[32]{0:T(128)} %get-tuple-element.18.base_ref, s32[1]{0:T(128)} %slice.21.live_ref, f32[32]{0:T(128)} %slice_reduce_fusion.weight_ref, bf16[32,64,4096]{2,1,0:T(8,128)(2,1)} %images.1.image_ref), custom_call_target="tpu_custom_call" | custom-call | tf_op jit(solution)/shard_map/placed/pallas_call | solution.py:173
  125.5 0.0 copy-start
  125.5 54.6 %spread.1 = bf16[256,4096]{1,0:T(8,128)(2,1)} custom-call(bf16[1024,1024]{1,0:T(8,128)(2,1)} %get-tuple-element.8.factor_ref, bf16[1024,4096]{1,0:T(8,128)(2,1)} %placed.1.grid_ref), custom_call_target="tpu_custom_call" | custom-call | tf_op jit(solution)/shard_map/spread/pallas_call | solution.py:549
  180.1 0.0 copy-done
  180.1 4.3 %convert_add_fusion = f32[256,4096]{1,0:T(8,128)} fusion(bf16[256,4096]{1,0:T(8,128)(2,1)} %spread.1, bf16[256,4096]{1,0:T(8,128)(2,1)S(1)} %copy-done), kind=kLoop, calls=%fused_computation | loop fusion | flops 3145728 | bytes 8388608 | tf_op jit(solution)/shard_map/add | solution.py:614
  (1 shorter events, 0.0 us)
Async XLA Ops:
  6.5 76.0 %all-gather.2.cloned.1.call-start = ((), (), s32[]{:S(2)}) async-start(), calls=%async_computation | async-start | bytes 10485760 | tf_op jit(solution)/shard_map/all_gather | solution.py:592
  56.0 2.7 %copy-start.1 = (s32[9]{0:T(128)}, s32[9]{0:T(128)S(1)}, u32[]{:S(2)}) copy-start(s32[9]{0:T(128)S(1)} %convert_reduce_fusion.1.start_ref) | copy-start | bytes 112
  125.5 54.6 %copy-start = (bf16[256,4096]{1,0:T(8,128)(2,1)S(1)}, bf16[256,4096]{1,0:T(8,128)(2,1)}, u32[]{:S(2)}) copy-start(bf16[256,4096]{1,0:T(8,128)(2,1)} %param.9) | copy-start | bytes 6291460
Sparse Core Ops, SparseCore 0:
  8.9 60.9 all-gather.1
